TPU v7x, 128 devices: a whole 4x4x4 slice. The times are simulated.
128 devices in a mesh: group: 32 (over x, z, core), shard: 4 (over y).
Axes of the slice: x: 4, y: 4, z: 4, core: 2. Of those that a mesh axis runs over, the one named last changes fastest.
Arguments:
- tokens: bfloat16 [32768, 1024], P(('group', 'shard')), may hold values from -6 to 6
- doc_lengths: int32 [128, 4], P(('group', 'shard')), may hold values from 1 to 128, 256 in all within a row
- cotangent: bfloat16 [32768, 1024], P(('group', 'shard')), may hold values from -6 to 6
- in_weight: float32 [1024, 3072], P(('group', 'shard')), may hold values from -0.1875 to 0.1875
- in_first: float32 [1024, 3072], P(('group', 'shard')), may hold values from -0.00015258789 to 0.00015258789
- in_second: float32 [1024, 3072], P(('group', 'shard')), may hold values from 1.6344143e-09 to 1.0896095e-08
- out_weight: float32 [1024, 1024], P(('group', 'shard')), may hold values from -0.1875 to 0.1875
- out_first: float32 [1024, 1024], P(('group', 'shard')), may hold values from -0.00015258789 to 0.00015258789
- out_second: float32 [1024, 1024], P(('group', 'shard')), may hold values from 1.6344143e-09 to 1.0896095e-08
- ffn_weight: float32 [1024, 9216], P(('group', 'shard')), may hold values from -0.1875 to 0.1875
- ffn_first: float32 [1024, 9216], P(('group', 'shard')), may hold values from -0.00015258789 to 0.00015258789
- ffn_second: float32 [1024, 9216], P(('group', 'shard')), may hold values from 1.6344143e-09 to 1.0896095e-08
- down_weight: float32 [4608, 1024], P(('group', 'shard')), may hold values from -0.09375 to 0.09375
- down_first: float32 [4608, 1024], P(('group', 'shard')), may hold values from -0.00015258789 to 0.00015258789
- down_second: float32 [4608, 1024], P(('group', 'shard')), may hold values from 1.6344143e-09 to 1.0896095e-08
- conv_weight: float32 [3, 1024], P(None, ('group', 'shard')), may hold values from -3.5 to 3.5
- conv_first: float32 [3, 1024], P(None, ('group', 'shard')), may hold values from -0.00048828125 to 0.00048828125
- conv_second: float32 [3, 1024], P(None, ('group', 'shard')), may hold values from 1.4709728e-08 to 9.806485e-08
- gains: float32 [2, 1024], P(None, ('group', 'shard')), may hold values from 0.3 to 3.3, as said below
- gains_first: float32 [2, 1024], P(None, ('group', 'shard')), may hold values from -0.00048828125 to 0.00048828125
- gains_second: float32 [2, 1024], P(None, ('group', 'shard')), may hold values from 1.4709728e-08 to 9.806485e-08
Outputs:
- output: bfloat16 [32768, 1024], P(('group', 'shard'))
- tokens_grad: float32 [32768, 1024], P(('group', 'shard'))
- grad_norm: float32 [], replicated
- new_in_weight: float32 [1024, 3072], P(('group', 'shard'))
- new_in_first: float32 [1024, 3072], P(('group', 'shard'))
- new_in_second: float32 [1024, 3072], P(('group', 'shard'))
- new_out_weight: float32 [1024, 1024], P(('group', 'shard'))
- new_out_first: float32 [1024, 1024], P(('group', 'shard'))
- new_out_second: float32 [1024, 1024], P(('group', 'shard'))
- new_ffn_weight: float32 [1024, 9216], P(('group', 'shard'))
- new_ffn_first: float32 [1024, 9216], P(('group', 'shard'))
- new_ffn_second: float32 [1024, 9216], P(('group', 'shard'))
- new_down_weight: float32 [4608, 1024], P(('group', 'shard'))
- new_down_first: float32 [4608, 1024], P(('group', 'shard'))
- new_down_second: float32 [4608, 1024], P(('group', 'shard'))
- new_conv_weight: float32 [3, 1024], P(None, ('group', 'shard'))
- new_conv_first: float32 [3, 1024], P(None, ('group', 'shard'))
- new_conv_second: float32 [3, 1024], P(None, ('group', 'shard'))
- new_gains: float32 [2, 1024], P(None, ('group', 'shard'))
- new_gains_first: float32 [2, 1024], P(None, ('group', 'shard'))
- new_gains_second: float32 [2, 1024], P(None, ('group', 'shard'))
Inputs may be any that keep to these rules, and one draw needn't show every extreme that they name: `doc_lengths`: each row holds the lengths of 4 documents that fill one sequence of 256 tokens; the largest is exactly 128. Positive gains.
All inputs are finite; a program needn't handle non-finite values.
Results may differ from a plain program's by a relative error of at most 0.022.
Values may be sent and summed in bfloat16 or wider, within the bound.
No kernel may reach another device: no remote copies, remote signals or barrier semaphores. Data moves between devices by JAX's collectives and lax.ppermute only.
A program may use at most 256 MiB of HBM per device.

v0:
```python
import jax
import jax.numpy as jnp
from jax import lax
from jax.sharding import PartitionSpec as P

D = 1024
FF = 4608
STEP = 10


eps_norm = 1e-05
beta_one = 0.9
beta_two = 0.95
adam_eps = 1e-08
clip_level = 1.0
rate_matrix = 0.03
rate_vector = 0.5
decay_matrix = 0.1


def delay_rows(values, offset):
    if offset == 0:
        return values
    return jnp.concatenate([jnp.zeros_like(values[:offset]), values[:-offset]], axis=0)


def advance_rows(values, offset):
    return jnp.concatenate([values[offset:], jnp.zeros_like(values[:offset])], axis=0)


def tap_masks(lengths, row_count):
    lengths = lengths.reshape(-1)
    ends = jnp.cumsum(lengths)
    starts = ends - lengths
    places = jnp.arange(row_count, dtype=jnp.int32)
    begin = jnp.max(jnp.where(starts[None, :] <= places[:, None], starts[None, :], 0), axis=1)
    return [(places - offset >= begin).astype(jnp.float32)[:, None] for offset in range(3)]


def gather_weights(pieces):
    return (
        lax.all_gather(pieces[0], ("group", "shard"), axis=0, tiled=True),
        lax.all_gather(pieces[1], ("group", "shard"), axis=0, tiled=True),
        lax.all_gather(pieces[2], ("group", "shard"), axis=0, tiled=True),
        lax.all_gather(pieces[3], ("group", "shard"), axis=0, tiled=True),
        lax.all_gather(pieces[4], ("group", "shard"), axis=1, tiled=True),
        lax.all_gather(pieces[5], ("group", "shard"), axis=1, tiled=True),
    )


def reduce_grads(grads):
    return (
        lax.psum_scatter(grads[0], ("group", "shard"), scatter_dimension=0, tiled=True),
        lax.psum_scatter(grads[1], ("group", "shard"), scatter_dimension=0, tiled=True),
        lax.psum_scatter(grads[2], ("group", "shard"), scatter_dimension=0, tiled=True),
        lax.psum_scatter(grads[3], ("group", "shard"), scatter_dimension=0, tiled=True),
        lax.psum_scatter(grads[4], ("group", "shard"), scatter_dimension=1, tiled=True),
        lax.psum_scatter(grads[5], ("group", "shard"), scatter_dimension=1, tiled=True),
    )


def adam_step(weight, first, second, grad, rate, decay):
    first = beta_one * first + (1.0 - beta_one) * grad
    second = beta_two * second + (1.0 - beta_two) * grad * grad
    mean_hat = first / (1.0 - beta_one**STEP)
    var_hat = second / (1.0 - beta_two**STEP)
    weight = weight - rate * (mean_hat / (jnp.sqrt(var_hat) + adam_eps) + decay * weight)
    return (weight, first, second)


def shards(
    tokens,
    doc_lengths,
    cotangent,
    in_weight,
    in_first,
    in_second,
    out_weight,
    out_first,
    out_second,
    ffn_weight,
    ffn_first,
    ffn_second,
    down_weight,
    down_first,
    down_second,
    conv_weight,
    conv_first,
    conv_second,
    gains,
    gains_first,
    gains_second,
):
    masters = (in_weight, out_weight, ffn_weight, down_weight, conv_weight, gains)
    in_full, out_full, ffn_full, down_full, taps_full, gains_full = gather_weights(
        tuple((master.astype(jnp.bfloat16) for master in masters))
    )
    row_count = tokens.shape[0]
    conv_taps = taps_full.astype(jnp.float32)
    gain_one = gains_full[0].astype(jnp.float32)
    gain_two = gains_full[1].astype(jnp.float32)
    masks = tap_masks(doc_lengths, row_count)
    values = tokens.astype(jnp.float32)
    inverse_one = lax.rsqrt(jnp.mean(values * values, axis=1, keepdims=True) + eps_norm)
    normed_one = (values * inverse_one * gain_one).astype(jnp.bfloat16)
    projected = jnp.dot(normed_one, in_full, preferred_element_type=jnp.float32)
    b_part = projected[:, :D]
    c_part = projected[:, D : 2 * D]
    v_part = projected[:, 2 * D :]
    mixed_in = b_part * v_part
    shifted = [delay_rows(mixed_in, offset) * masks[offset] for offset in range(3)]
    conv_out = conv_taps[0] * shifted[0] + conv_taps[1] * shifted[1] + conv_taps[2] * shifted[2]
    gated = (c_part * conv_out).astype(jnp.bfloat16)
    middle = values + jnp.dot(gated, out_full, preferred_element_type=jnp.float32)
    inverse_two = lax.rsqrt(jnp.mean(middle * middle, axis=1, keepdims=True) + eps_norm)
    normed_two = (middle * inverse_two * gain_two).astype(jnp.bfloat16)
    both_parts = jnp.dot(normed_two, ffn_full, preferred_element_type=jnp.float32)
    gate_pre = both_parts[:, :FF]
    up_pre = both_parts[:, FF:]
    sigmoid_gate = jax.nn.sigmoid(gate_pre)
    silu_gate = gate_pre * sigmoid_gate
    product = (silu_gate * up_pre).astype(jnp.bfloat16)
    output = (middle + jnp.dot(product, down_full, preferred_element_type=jnp.float32)).astype(
        jnp.bfloat16
    )
    out_grad = cotangent.astype(jnp.float32)
    d_product = jnp.dot(cotangent, down_full.T, preferred_element_type=jnp.float32)
    grad_down = jnp.dot(product.T, cotangent, preferred_element_type=jnp.float32)
    d_gate = d_product * up_pre * sigmoid_gate * (1.0 + gate_pre * (1.0 - sigmoid_gate))
    d_up = d_product * silu_gate
    d_both = jnp.concatenate([d_gate, d_up], axis=1).astype(jnp.bfloat16)
    grad_ffn = jnp.dot(normed_two.T, d_both, preferred_element_type=jnp.float32)
    d_normed_two = jnp.dot(d_both, ffn_full.T, preferred_element_type=jnp.float32)
    grad_gain_two = jnp.sum(d_normed_two * middle * inverse_two, axis=0)
    scaled_two = d_normed_two * gain_two
    d_middle = (
        out_grad
        + inverse_two * scaled_two
        - middle * inverse_two**3 * jnp.mean(scaled_two * middle, axis=1, keepdims=True)
    )
    d_middle_low = d_middle.astype(jnp.bfloat16)
    grad_out = jnp.dot(gated.T, d_middle_low, preferred_element_type=jnp.float32)
    d_gated = jnp.dot(d_middle_low, out_full.T, preferred_element_type=jnp.float32)
    d_c_part = d_gated * conv_out
    d_conv = d_gated * c_part
    grad_taps = jnp.stack([jnp.sum(d_conv * shifted[offset], axis=0) for offset in range(3)])
    d_mixed = conv_taps[0] * d_conv * masks[0]
    for offset in range(1, 3):
        d_mixed = d_mixed + conv_taps[offset] * advance_rows(d_conv * masks[offset], offset)
    d_proj = jnp.concatenate([d_mixed * v_part, d_c_part, d_mixed * b_part], axis=1).astype(
        jnp.bfloat16
    )
    grad_in = jnp.dot(normed_one.T, d_proj, preferred_element_type=jnp.float32)
    d_normed_one = jnp.dot(d_proj, in_full.T, preferred_element_type=jnp.float32)
    grad_gain_one = jnp.sum(d_normed_one * values * inverse_one, axis=0)
    scaled_one = d_normed_one * gain_one
    tokens_grad = (
        d_middle
        + inverse_one * scaled_one
        - values * inverse_one**3 * jnp.mean(scaled_one * values, axis=1, keepdims=True)
    )
    grad_gains = jnp.stack([grad_gain_one, grad_gain_two])
    owned = reduce_grads((grad_in, grad_out, grad_ffn, grad_down, grad_taps, grad_gains))
    local_squares = jnp.float32(0.0)
    for grad in owned:
        local_squares = local_squares + jnp.sum(grad * grad)
    squares = lax.psum(local_squares, ("group", "shard"))
    grad_norm = jnp.sqrt(squares)
    factor = jnp.minimum(1.0, clip_level / grad_norm)
    states = (
        (in_weight, in_first, in_second),
        (out_weight, out_first, out_second),
        (ffn_weight, ffn_first, ffn_second),
        (down_weight, down_first, down_second),
        (conv_weight, conv_first, conv_second),
        (gains, gains_first, gains_second),
    )
    results = []
    for index in range(6):
        rate = rate_matrix if index < 4 else rate_vector
        decay = decay_matrix if index < 4 else 0.0
        weight, first, second = states[index]
        results.extend(adam_step(weight, first, second, owned[index] * factor, rate, decay))
    return (
        output,
        tokens_grad,
        grad_norm,
        results[0],
        results[1],
        results[2],
        results[3],
        results[4],
        results[5],
        results[6],
        results[7],
        results[8],
        results[9],
        results[10],
        results[11],
        results[12],
        results[13],
        results[14],
        results[15],
        results[16],
        results[17],
    )


def solution(mesh):
    return jax.shard_map(
        shards,
        mesh=mesh,
        in_specs=(
            P(("group", "shard"), None),
            P(("group", "shard"), None),
            P(("group", "shard"), None),
            P(("group", "shard"), None),
            P(("group", "shard"), None),
            P(("group", "shard"), None),
            P(("group", "shard"), None),
            P(("group", "shard"), None),
            P(("group", "shard"), None),
            P(("group", "shard"), None),
            P(("group", "shard"), None),
            P(("group", "shard"), None),
            P(("group", "shard"), None),
            P(("group", "shard"), None),
            P(("group", "shard"), None),
            P(None, ("group", "shard")),
            P(None, ("group", "shard")),
            P(None, ("group", "shard")),
            P(None, ("group", "shard")),
            P(None, ("group", "shard")),
            P(None, ("group", "shard")),
        ),
        out_specs=(
            P(("group", "shard"), None),
            P(("group", "shard"), None),
            P(),
            P(("group", "shard"), None),
            P(("group", "shard"), None),
            P(("group", "shard"), None),
            P(("group", "shard"), None),
            P(("group", "shard"), None),
            P(("group", "shard"), None),
            P(("group", "shard"), None),
            P(("group", "shard"), None),
            P(("group", "shard"), None),
            P(("group", "shard"), None),
            P(("group", "shard"), None),
            P(("group", "shard"), None),
            P(None, ("group", "shard")),
            P(None, ("group", "shard")),
            P(None, ("group", "shard")),
            P(None, ("group", "shard")),
            P(None, ("group", "shard")),
            P(None, ("group", "shard")),
        ),
        check_vma=False,
    )
```

profile of v0, /device:TPU:0, one launch (start us, length us, event | category | flops | bytes accessed | tf_op | source)
XLA Modules:
  0.0 1583.5 jit_solution(12061909550447390739)
XLA Ops:
  7.2 1.5 convert_element_type.75
  8.8 1.4 convert_element_type.82
  10.3 1.6 convert_bitcast_fusion
  11.9 1.6 convert_element_type.84
  13.6 0.7 convert_bitcast_fusion.2
  14.3 53.0 %all-gather = bf16[128,8,2]{1,2,0:T(2,128)(2,1)S(1)} all-gather(bf16[1,8,2]{1,2,0:T(2,128)(2,1)S(1)} %convert_bitcast_fusion.2), channel_id=1, replica_groups=mesh['group'=32,'shard'=4] {'group','shard'}, dimensions={0}, use_global_device_ids=true | all-gather | bytes 4128 | tf_op jit(solution)/shard_map/all_gather | solution.py:47
  67.5 0.7 convert_bitcast_fusion.1
  68.2 53.4 %all-gather.1 = bf16[128,8,3]{1,2,0:T(4,128)(2,1)S(1)} all-gather(bf16[1,8,3]{1,2,0:T(4,128)(2,1)S(1)} %convert_bitcast_fusion.1), channel_id=1, replica_groups=mesh['group'=32,'shard'=4] {'group','shard'}, dimensions={0}, use_global_device_ids=true | all-gather | bytes 6192 | tf_op jit(solution)/shard_map/all_gather | solution.py:46
  121.9 0.8 reduce-window_clone.1
  122.8 0.7 subtract_bitcast_fusion
  123.5 1.2 fusion.5
  124.8 4.8 fusion.22
  129.8 1.5 copy-done
  131.3 1.6 multiply_convert_fusion.7
  132.9 15.9 %all-gather.10.cloned.1.call-done = bf16[1024,1024]{1,0:T(8,128)(2,1)} async-done(((bf16[8,1024]{1,0:T(8,128)(2,1)}), bf16[1024,1024]{1,0:T(8,128)(2,1)}) %all-gather.10.cloned.1.call-update) | async-done | bytes 2097168 | tf_op jit(solution)/shard_map/all_gather | solution.py:43
  148.8 2.4 multiply_reduce_fusion.5
  151.2 70.4 %all-gather.14.cloned.1.call-done = bf16[128,36,1024]{2,1,0:T(8,128)(2,1)} async-done(((bf16[1,36,1024]{2,1,0:T(8,128)(2,1)}), bf16[128,36,1024]{2,1,0:T(8,128)(2,1)}) %all-gather.14.cloned.1.call-update) | async-done | bytes 9437200 | tf_op jit(solution)/shard_map/all_gather | solution.py:45
  221.6 13.1 reshape.115
  234.7 71.8 %all-gather.12.cloned.1.call-done = bf16[1024,9216]{1,0:T(8,128)(2,1)} async-done(((bf16[8,9216]{1,0:T(8,128)(2,1)}), bf16[1024,9216]{1,0:T(8,128)(2,1)}) %all-gather.12.cloned.1.call-update) | async-done | bytes 18874384 | tf_op jit(solution)/shard_map/all_gather | solution.py:44
  306.6 9.1 fusion.32
  315.7 13.0 multiply_convert_fusion.1
  328.7 11.4 multiply_reduce_fusion
  340.1 1.6 multiply_subtract_fusion
  341.7 2.8 fusion.16
  344.9 3.4 multiply_reduce_fusion.3
  349.9 6.4 fusion.13
  356.4 17.3 %fusion.2 = f32[1024,9216]{1,0:T(8,128)} fusion(bf16[256,4608]{1,0:T(8,128)(2,1)} %get-tuple-element.54, bf16[256,4608]{1,0:T(8,128)(2,1)} %get-tuple-element.53, f32[256,1024]{1,0:T(8,128)S(1)} %get-tuple-element.70, f32[1024]{0:T(1024)S(1)} %bitcast.55, f32[256]{0:T(256)S(1)} %get-tuple-element.65), kind=kOutput, calls=%fused_computation.6 | convolution fusion | flops 4842061824 | bytes 43521024 | tf_op jit(solution)/shard_map/dot_general | solution.py:132
  373.7 10.8 fusion.40
  384.5 370.4 %fusion = f32[40,1024]{1,0:T(8,128)S(1)} fusion(f32[4608,1024]{1,0:T(8,128)} %fusion.40), kind=kCustom, calls=%all-reduce-scatter | all-reduce-scatter fusion | flops 5242881 | bytes 19038208
  755.0 1.6 collective-permute-start.11
  756.6 1.4 collective-permute-start.10
  758.0 2.0 collective-permute-start.9
  760.0 1.9 collective-permute-start.8
  761.9 1.5 collective-permute-start.12
  763.5 7.8 fusion.4
  771.3 2.9 fusion.12
  774.2 1.4 collective-permute-start.7
  775.7 1.3 collective-permute-start.6
  777.7 1.3 collective-permute-start.5
  779.0 76.4 %all-reduce.8 = (f32[3,1024]{1,0:T(4,128)S(1)}, f32[2,1024]{1,0:T(2,128)S(1)}) all-reduce(f32[3,1024]{1,0:T(4,128)S(1)} %pad_maximum_fusion.6, f32[2,1024]{1,0:T(2,128)S(1)} %pad_maximum_fusion.7), channel_id=6, replica_groups=mesh['group'=32,'shard'=4] {'group','shard'}, use_global_device_ids=true, to_apply=%region_17.18.clone | all-reduce | flops 5120 | bytes 40960
  855.4 0.7 multiply_reduce_fusion.11
  856.1 0.7 multiply_reduce_fusion.10
  856.7 1.7 collective-permute-start.4
  858.5 2.7 collective-permute-start.3
  861.2 4.3 collective-permute-start.2
  865.5 2.3 collective-permute-start.1
  867.7 3.4 collective-permute-start
  872.6 0.7 copy-done.24
  873.2 2.7 collective-permute-done
  876.0 22.3 %concatenate.26 = f32[548,1024]{1,0:T(8,128)} concatenate(f32[28,1024]{1,0:T(8,128)} %copy-done.25, f32[40,1024]{1,0:T(8,128)S(1)} %collective-permute-done.11, f32[40,1024]{1,0:T(8,128)} %copy-done.18, f32[40,1024]{1,0:T(8,128)} %collective-permute-done.9, f32[40,1024]{1,0:T(8,128)} %collective-permute-done.8, f32[40,1024]{1,0:T(8,128)S(1)} %collective-permute-done.7, ...), dimensions={0} | concatenate | bytes 4489216
  898.3 1.6 multiply_reduce_fusion.7
  899.9 90.7 %reduce-scatter.10.cloned.1.call-done = f32[8,1024]{1,0:T(8,128)} async-done(((f32[1024,1024]{1,0:T(8,128)}), f32[8,1024]{1,0:T(8,128)}) %reduce-scatter.10.cloned.1.call-update) | async-done | bytes 32784 | tf_op jit(solution)/shard_map/reduce_scatter | solution.py:54
  990.6 1.4 multiply_reduce_fusion.9
  992.1 220.3 %reduce-scatter.8.cloned.1.call-done = f32[8,3072]{1,0:T(8,128)} async-done(((f32[1024,3072]{1,0:T(8,128)}), f32[8,3072]{1,0:T(8,128)}) %reduce-scatter.8.cloned.1.call-update) | async-done | bytes 98320 | tf_op jit(solution)/shard_map/reduce_scatter | solution.py:53
  1212.3 1.6 multiply_reduce_fusion.8
  1215.2 281.8 %reduce-scatter.12.cloned.1.call-done = f32[8,9216]{1,0:T(8,128)} async-done(((f32[1024,9216]{1,0:T(8,128)}), f32[8,9216]{1,0:T(8,128)}) %reduce-scatter.12.cloned.1.call-update) | async-done | bytes 294928 | tf_op jit(solution)/shard_map/reduce_scatter | solution.py:55
  1497.1 1.7 multiply_reduce_fusion.6
  1501.4 2.5 fusion.9
  1503.9 62.7 %psum.7 = f32[]{:T(128)} all-reduce(f32[]{:T(128)S(6)} %add.199), channel_id=1, replica_groups=mesh['group'=32,'shard'=4] {'group','shard'}, use_global_device_ids=true, to_apply=%region_23.24 | all-reduce | flops 1 | bytes 8 | tf_op jit(solution)/shard_map/psum | solution.py:167
  1567.4 2.0 multiply_subtract_fusion.2
  1569.3 1.4 multiply_subtract_fusion.5
  1570.7 1.4 multiply_subtract_fusion.6
  1572.8 1.7 multiply_subtract_fusion.3
  1574.5 1.1 multiply_subtract_fusion.1
  (120 shorter events, 5.9 us)
Async XLA Ops:
  7.2 117.6 %all-gather.8.cloned.1.call-start = ((), (), s32[]{:S(2)}) async-start(), calls=%async_computation.3 | async-start | bytes 6340608 | tf_op jit(solution)/shard_map/all_gather | solution.py:42
  8.8 140.0 %all-gather.10.cloned.1.call-start = ((), (), s32[]{:S(2)}) async-start(), calls=%async_computation.4 | async-start | bytes 2113536 | tf_op jit(solution)/shard_map/all_gather | solution.py:43
  10.2 211.4 %all-gather.14.cloned.1.call-start = ((), (), s32[]{:S(2)}) async-start(), calls=%async_computation.9 | async-start | bytes 10567680 | tf_op jit(solution)/shard_map/all_gather | solution.py:45
  11.9 294.7 %all-gather.12.cloned.1.call-start = ((), (), s32[]{:S(2)}) async-start(), calls=%async_computation.5 | async-start | bytes 19021824 | tf_op jit(solution)/shard_map/all_gather | solution.py:44
  13.6 977.0 %reduce-scatter.10.cloned.1.call-start = ((), (), s32[]{:S(2)}) async-start(), calls=%async_computation.7 | async-start | bytes 4227072 | tf_op jit(solution)/shard_map/reduce_scatter | solution.py:54
  129.7 1.6 copy-start
  129.7 19.1 %copy-start.2 = (bf16[256,1024]{1,0:T(8,128)(2,1)S(1)}, bf16[256,1024]{1,0:T(8,128)(2,1)}, u32[]{:S(2)}) copy-start(bf16[256,1024]{1,0:T(8,128)(2,1)} %param.21) | copy-start | bytes 1572868
  132.9 101.9 %copy-start.4 = (bf16[256,1024]{1,0:T(8,128)(2,1)}, bf16[256,1024]{1,0:T(8,128)(2,1)S(1)}, u32[]{:S(2)}) copy-start(bf16[256,1024]{1,0:T(8,128)(2,1)S(1)} %get-tuple-element.51) | copy-start | bytes 1572868
  306.6 9.1 copy-start.8
  328.7 12.9 copy-start.5
  344.5 867.8 %reduce-scatter.8.cloned.1.call-start = ((), (), s32[]{:S(2)}) async-start(), calls=%async_computation.6 | async-start | bytes 12681216 | tf_op jit(solution)/shard_map/reduce_scatter | solution.py:53
  344.9 3.8 copy-start.1
  348.4 0.9 copy-start.6
  348.7 1.2 copy-start.3
  349.1 0.8 copy-start.9
  356.4 1140.7 %reduce-scatter.12.cloned.1.call-start = ((), (), s32[]{:S(2)}) async-start(), calls=%async_computation.8 | async-start | bytes 38043648 | tf_op jit(solution)/shard_map/reduce_scatter | solution.py:55
  755.0 16.3 %slice-start = ((s8[6291456]{0:T(1024)(128)(4,1)}), s8[4194304]{0:T(1024)(128)(4,1)S(1)}, s32[]{:S(2)}) async-start(s8[6291456]{0:T(1024)(128)(4,1)} %bitcast.73), calls=%async_computation.10 | async-start | bytes 8388608
  755.0 16.3 %copy-start.7 = (bf16[256,1024]{1,0:T(8,128)(2,1)S(1)}, bf16[256,1024]{1,0:T(8,128)(2,1)}, u32[]{:S(2)}) copy-start(bf16[256,1024]{1,0:T(8,128)(2,1)} %copy-done.6) | copy-start | bytes 1572868
  755.0 16.3 %copy-start.10 = (bf16[256,1024]{1,0:T(8,128)(2,1)S(1)}, bf16[256,1024]{1,0:T(8,128)(2,1)}, u32[]{:S(2)}) copy-start(bf16[256,1024]{1,0:T(8,128)(2,1)} %copy-done.9) | copy-start | bytes 1572868
  755.0 16.3 %slice-start.1 = ((s8[6291456]{0:T(1024)(128)(4,1)}), s8[2097152]{0:T(1024)(128)(4,1)S(1)}, s32[]{:S(2)}) async-start(s8[6291456]{0:T(1024)(128)(4,1)} %bitcast.73), calls=%async_computation.11 | async-start | bytes 4194304
  755.0 20.7 %collective-permute-start.11 = (f32[40,1024]{1,0:T(8,128)S(1)}, f32[40,1024]{1,0:T(8,128)S(1)}, u32[]{:S(2)}, u32[]{:S(2)}) collective-permute-start(f32[40,1024]{1,0:T(8,128)S(1)} %fusion), channel_id=1, source_target_pairs={{0,12},{1,13},{2,14},{3,15},{4,16},{5,17},{6,18},{7,19},{8,20},{9,... | collective-permute-start | bytes 491528
  756.6 20.4 %collective-permute-start.10 = (f32[40,1024]{1,0:T(8,128)S(1)}, f32[40,1024]{1,0:T(8,128)S(1)}, u32[]{:S(2)}, u32[]{:S(2)}) collective-permute-start(f32[40,1024]{1,0:T(8,128)S(1)} %fusion), channel_id=1, source_target_pairs={{0,11},{1,12},{2,13},{3,14},{4,15},{5,16},{6,17},{7,18},{8,19},{9,... | collective-permute-start | bytes 491528
  758.0 98.7 %collective-permute-start.9 = (f32[40,1024]{1,0:T(8,128)S(1)}, f32[40,1024]{1,0:T(8,128)}, u32[]{:S(2)}, u32[]{:S(2)}) collective-permute-start(f32[40,1024]{1,0:T(8,128)S(1)} %fusion), channel_id=1, source_target_pairs={{0,10},{1,11},{2,12},{3,13},{4,14},{5,15},{6,16},{7,17},{8,18},{9,... | collective-permute-start | bytes 491528
  760.0 98.5 %collective-permute-start.8 = (f32[40,1024]{1,0:T(8,128)S(1)}, f32[40,1024]{1,0:T(8,128)}, u32[]{:S(2)}, u32[]{:S(2)}) collective-permute-start(f32[40,1024]{1,0:T(8,128)S(1)} %fusion), channel_id=1, source_target_pairs={{0,9},{1,10},{2,11},{3,12},{4,13},{5,14},{6,15},{7,16},{8,17},{9,1... | collective-permute-start | bytes 491528
  761.9 12.3 collective-permute-start.12
  774.2 793.1 %copy-start.13 = (f32[36,1024]{1,0:T(8,128)S(1)}, f32[36,1024]{1,0:T(8,128)}, u32[]{:S(2)}) copy-start(f32[36,1024]{1,0:T(8,128)} %param.33) | copy-start | bytes 442372
  774.2 4.7 copy-start.25
  774.2 86.9 %collective-permute-start.7 = (f32[40,1024]{1,0:T(8,128)S(1)}, f32[40,1024]{1,0:T(8,128)S(1)}, u32[]{:S(2)}, u32[]{:S(2)}) collective-permute-start(f32[40,1024]{1,0:T(8,128)S(1)} %fusion), channel_id=1, source_target_pairs={{0,8},{1,9},{2,10},{3,11},{4,12},{5,13},{6,14},{7,15},{8,16},{9,17... | collective-permute-start | bytes 491528
  775.7 89.7 %collective-permute-start.6 = (f32[40,1024]{1,0:T(8,128)S(1)}, f32[40,1024]{1,0:T(8,128)S(1)}, u32[]{:S(2)}, u32[]{:S(2)}) collective-permute-start(f32[40,1024]{1,0:T(8,128)S(1)} %fusion), channel_id=1, source_target_pairs={{0,7},{1,8},{2,9},{3,10},{4,11},{5,12},{6,13},{7,14},{8,15},{9,16}... | collective-permute-start | bytes 491528
  777.0 0.7 copy-start.18
  777.7 90.1 %collective-permute-start.5 = (f32[40,1024]{1,0:T(8,128)S(1)}, f32[40,1024]{1,0:T(8,128)S(1)}, u32[]{:S(2)}, u32[]{:S(2)}) collective-permute-start(f32[40,1024]{1,0:T(8,128)S(1)} %fusion), channel_id=1, source_target_pairs={{0,6},{1,7},{2,8},{3,9},{4,10},{5,11},{6,12},{7,13},{8,14},{9,15},... | collective-permute-start | bytes 491528
  855.4 15.7 copy-start.32
  855.4 136.7 %copy-start.31 = (f32[3,1024]{1,0:T(4,128)}, f32[3,1024]{1,0:T(4,128)S(1)}, u32[]{:S(2)}) copy-start(f32[3,1024]{1,0:T(4,128)S(1)} %get-tuple-element.28) | copy-start | bytes 36868
  856.7 15.0 collective-permute-start.4
  858.5 13.3 collective-permute-start.3
  861.2 10.6 collective-permute-start.2
  865.4 5.7 copy-start.19
  865.5 6.6 collective-permute-start.1
  867.7 3.4 copy-start.20
  867.7 8.2 collective-permute-start
  871.7 697.6 %copy-start.30 = (f32[3,8]{1,0:T(4,128)S(1)}, f32[3,8]{1,0:T(4,128)}, u32[]{:S(2)}) copy-start(f32[3,8]{1,0:T(4,128)} %param.36) | copy-start | bytes 292
  871.7 700.4 %copy-start.26 = (f32[8,1024]{1,0:T(8,128)S(1)}, f32[8,1024]{1,0:T(8,128)}, u32[]{:S(2)}) copy-start(f32[8,1024]{1,0:T(8,128)} %param.27) | copy-start | bytes 98308
  871.7 700.4 %copy-start.28 = (f32[8,1024]{1,0:T(8,128)S(1)}, f32[8,1024]{1,0:T(8,128)}, u32[]{:S(2)}) copy-start(f32[8,1024]{1,0:T(8,128)} %param.28) | copy-start | bytes 98308
  871.7 700.4 %copy-start.29 = (f32[8,1024]{1,0:T(8,128)S(1)}, f32[8,1024]{1,0:T(8,128)}, u32[]{:S(2)}) copy-start(f32[8,1024]{1,0:T(8,128)} %param.29) | copy-start | bytes 98308
  871.7 701.1 %copy-start.14 = (f32[8,3072]{1,0:T(8,128)S(1)}, f32[8,3072]{1,0:T(8,128)}, u32[]{:S(2)}) copy-start(f32[8,3072]{1,0:T(8,128)} %param.24) | copy-start | bytes 294916
  871.7 702.8 %copy-start.11 = (f32[8,9216]{1,0:T(8,128)S(1)}, f32[8,9216]{1,0:T(8,128)}, u32[]{:S(2)}) copy-start(f32[8,9216]{1,0:T(8,128)} %param.30) | copy-start | bytes 884740
  871.7 702.8 %copy-start.16 = (f32[8,9216]{1,0:T(8,128)S(1)}, f32[8,9216]{1,0:T(8,128)}, u32[]{:S(2)}) copy-start(f32[8,9216]{1,0:T(8,128)} %param.31) | copy-start | bytes 884740
  871.8 702.7 %copy-start.17 = (f32[8,9216]{1,0:T(8,128)S(1)}, f32[8,9216]{1,0:T(8,128)}, u32[]{:S(2)}) copy-start(f32[8,9216]{1,0:T(8,128)} %param.32) | copy-start | bytes 884740
  871.8 0.7 copy-start.21
  871.8 0.7 copy-start.22
  871.8 0.7 copy-start.23
  872.6 0.7 copy-start.24
  990.6 581.5 %copy-start.27 = (f32[8,1024]{1,0:T(8,128)S(1)}, f32[8,1024]{1,0:T(8,128)}, u32[]{:S(2)}) copy-start(f32[8,1024]{1,0:T(8,128)} %reduce-scatter.10.cloned.1.call-done) | copy-start | bytes 98308
  1212.3 360.5 %copy-start.15 = (f32[8,3072]{1,0:T(8,128)S(1)}, f32[8,3072]{1,0:T(8,128)}, u32[]{:S(2)}) copy-start(f32[8,3072]{1,0:T(8,128)} %reduce-scatter.8.cloned.1.call-done) | copy-start | bytes 294916
  1497.1 77.4 %copy-start.12 = (f32[8,9216]{1,0:T(8,128)S(1)}, f32[8,9216]{1,0:T(8,128)}, u32[]{:S(2)}) copy-start(f32[8,9216]{1,0:T(8,128)} %reduce-scatter.12.cloned.1.call-done) | copy-start | bytes 884740
Sparse Core Ops, SparseCore 0:
  11.7 70.6 all-gather.7
  85.9 62.8 all-gather.9
  152.5 69.0 all-gather.13
  225.1 81.4 all-gather.11
  344.6 645.9 reduce-scatter.9
  996.2 216.0 reduce-scatter.7
  1218.7 278.3 reduce-scatter.11
where the time goes:
time: 1590 us; the launch traced here: 1580 us
  waiting for transfers between devices  754 us (47%)
  blocking collectives  616 us (39%)
  matrix products  92.2 us (6%)
  local copies, waits for them, and re-layouts  40.2 us (3%)
  other arithmetic  33.3 us (2%)
  starting transfers between devices  27.3 us (2%)
  between operations  20.5 us (1%)
    unnamed x2, blocking collectives  447 us
    reduce_scatter x1, waiting for transfers between devices, reduce_grads(): lax.psum_scatter(grads[2], ('group', 'shard'), scatter_dimension=0, tiled...  282 us
    reduce_scatter x1, waiting for transfers between devices, reduce_grads(): lax.psum_scatter(grads[0], ('group', 'shard'), scatter_dimension=0, tiled...  220 us
    reduce_scatter x1, waiting for transfers between devices, reduce_grads(): lax.psum_scatter(grads[1], ('group', 'shard'), scatter_dimension=0, tiled...  90.7 us
    all_gather x1, waiting for transfers between devices, gather_weights(): lax.all_gather(pieces[2], ('group', 'shard'), axis=0, tiled=True)  71.8 us
    all_gather x1, waiting for transfers between devices, gather_weights(): lax.all_gather(pieces[3], ('group', 'shard'), axis=0, tiled=True)  70.4 us
    psum x1, blocking collectives, shards(): squares = lax.psum(local_squares, ('group', 'shard'))  62.7 us
    all_gather x1, blocking collectives, gather_weights(): lax.all_gather(pieces[4], ('group', 'shard'), axis=1, tiled=True)  53.4 us
  transfers between devices with their start and end apart: 20, of which 8 were waited for; matrix products, arithmetic and copies ran while one was open for 30% of the time, Pallas kernels for 0%

commit v1 on v0

v1 whole, which is shorter than its diff:
```python
import jax
import jax.numpy as jnp
from jax import lax
from jax.sharding import Mesh
from jax.sharding import PartitionSpec as P

D = 1024
FF = 4608
STEP = 10
TOK = 256
CH = 512
HID = 2304


eps_norm = 1e-05
beta_one = 0.9
beta_two = 0.95
adam_eps = 1e-08
clip_level = 1.0
rate_matrix = 0.03
rate_vector = 0.5
decay_matrix = 0.1

BF = jnp.bfloat16
F32 = jnp.float32
AXES = ("x", "z", "core", "y")


def dot(left, right):
    return jnp.dot(left, right, preferred_element_type=F32)


def dot_tn(left, right):
    return lax.dot_general(left, right, (((0,), (0,)), ((), ())), preferred_element_type=F32)


def dot_nt(left, right):
    return lax.dot_general(left, right, (((1,), (1,)), ((), ())), preferred_element_type=F32)


def ring_pairs(axis):
    pairs = []
    for place in range(4):
        for core in range(2):
            target = (place + (1 if core == 0 else -1)) % 4
            if axis == "y":
                pairs.append((core * 4 + place, core * 4 + target))
            else:
                pairs.append((place * 2 + core, target * 2 + core))
    return pairs


def hop(value, axis):
    names = ("core", "y") if axis == "y" else (axis, "core")
    return lax.ppermute(value, names, ring_pairs(axis))


def swap(value):
    return lax.ppermute(value, "core", [(0, 1), (1, 0)])


def place_back(axis, steps):
    core = lax.axis_index("core")
    sign = 1 - 2 * core
    return lax.rem(lax.axis_index(axis) - steps * sign + 8, 4)


def gather_ring(block, axis):
    stacked = jnp.zeros((4,) + block.shape, block.dtype)
    for step in range(4):
        if step:
            block = hop(block, axis)
        index = place_back(axis, step)
        stacked = lax.dynamic_update_slice(stacked, block[None], (index,) + (0,) * block.ndim)
    return stacked


def scatter_ring(blocks, axis, dim):
    def own(step):
        return lax.dynamic_index_in_dim(blocks, place_back(axis, step), dim, keepdims=False)

    moving = own(1)
    for step in (2, 3, 4):
        arrived = hop(moving, axis)
        moving = (arrived.astype(F32) + own(step % 4).astype(F32)).astype(BF)
    return moving


def sum_all(value, names):
    for name in names:
        if name == "core":
            value = value + swap(value)
        else:
            others = [
                lax.ppermute(value, name, [(i, (i + shift) % 4) for i in range(4)])
                for shift in (1, 2, 3)
            ]
            value = (value + others[1]) + (others[0] + others[2])
    return value


def split_cols(shard, groups, width):
    rows = shard.shape[0]
    parts = shard.reshape(rows, groups, 16, 2, width)
    return [parts[:, :, :, core, :].reshape(rows, groups * 16 * width) for core in range(2)]


def join_cols(halves, groups, width):
    rows = halves[0].shape[0]
    parts = [half.reshape(rows, groups, 16, 1, width) for half in halves]
    return jnp.concatenate(parts, axis=3).reshape(rows, groups * 32 * width)


def pick(core, zero, one):
    return jnp.where(core == 0, zero, one)


def delay_rows(values, offset):
    if offset == 0:
        return values
    return jnp.concatenate([jnp.zeros_like(values[:, :offset]), values[:, :-offset]], axis=1)


def advance_rows(values, offset):
    if offset == 0:
        return values
    return jnp.concatenate([values[:, offset:], jnp.zeros_like(values[:, :offset])], axis=1)


def tap_masks(lengths):
    ends = jnp.cumsum(lengths, axis=1)
    starts = ends - lengths
    places = jnp.arange(TOK, dtype=jnp.int32)
    begin = jnp.max(
        jnp.where(starts[:, None, :] <= places[None, :, None], starts[:, None, :], 0), axis=2
    )
    return [(places[None, :] - offset >= begin).astype(F32)[:, :, None] for offset in range(3)]


def adam_step(weight, first, second, grad, rate, decay):
    first = beta_one * first + (1.0 - beta_one) * grad
    second = beta_two * second + (1.0 - beta_two) * grad * grad
    mean_hat = first / (1.0 - beta_one**STEP)
    var_hat = second / (1.0 - beta_two**STEP)
    weight = weight - rate * (mean_hat / (jnp.sqrt(var_hat) + adam_eps) + decay * weight)
    return (weight, first, second)


def gather_weights(core, in_weight, out_weight, ffn_weight, down_weight, conv_weight, gains):
    in_halves = split_cols(in_weight.astype(BF), 3, 32)
    ffn_halves = split_cols(ffn_weight.astype(BF), 2, 144)
    gains_low = gains.astype(BF)
    keep = jnp.concatenate([pick(core, *in_halves), pick(core, *ffn_halves)], axis=1)
    send = jnp.concatenate([pick(core, *in_halves[::-1]), pick(core, *ffn_halves[::-1])], axis=1)
    came = swap(send)
    gains_came = swap(gains_low)
    rows = (pick(core, keep, came), pick(core, came, keep))
    gain_rows = (pick(core, gains_low, gains_came), pick(core, gains_came, gains_low))
    small = jnp.concatenate(
        [conv_weight.astype(BF), gain_rows[0], gain_rows[1], jnp.zeros((1, 8), BF)], axis=0
    )
    small = jnp.pad(small, ((0, 0), (0, 120)))
    out_rows = out_weight.astype(BF)

    def in_part(index):
        return [row[:, index * CH : (index + 1) * CH] for row in rows]

    def ffn_part(index):
        return [row[:, 3 * CH + index * HID : 3 * CH + (index + 1) * HID] for row in rows]

    conv_a = jnp.concatenate(in_part(0) + [out_rows[:, :384]], axis=1)
    conv_b = jnp.concatenate(in_part(1) + [out_rows[:, 384:768]], axis=1)
    conv_c = jnp.concatenate(in_part(2) + [out_rows[:, 768:], small], axis=1)
    gate = jnp.concatenate(ffn_part(0), axis=1)
    up = jnp.concatenate(ffn_part(1), axis=1)
    conv_a = gather_ring(gather_ring(gather_ring(conv_a, "y"), "z"), "x")
    conv_b = gather_ring(gather_ring(gather_ring(conv_b, "x"), "y"), "z")
    conv_c = gather_ring(gather_ring(gather_ring(conv_c, "z"), "x"), "y")
    conv_a = conv_a.transpose(0, 1, 2, 3, 4)
    conv_b = conv_b.transpose(2, 0, 1, 3, 4)
    conv_c = conv_c.transpose(1, 2, 0, 3, 4)

    def feature_rows(value, width):
        split = value.reshape(4, 4, 4, 8, 2, width).transpose(0, 1, 4, 2, 3, 5)
        return split.reshape(D, width)

    in_full = jnp.concatenate(
        [feature_rows(conv[..., : 2 * CH], CH) for conv in (conv_a, conv_b, conv_c)], axis=1
    )
    out_full = jnp.concatenate(
        [conv_a[..., 1024:], conv_b[..., 1024:], conv_c[..., 1024:1280]], axis=-1
    ).reshape(CH, D)
    small = conv_c[..., 1280:1288].astype(F32)
    taps = small[:, :, :, 0:3].transpose(3, 0, 1, 2, 4).reshape(3, CH)
    gain_full = small[:, :, :, 3:7].reshape(4, 4, 4, 2, 2, 8)
    gain_full = gain_full.transpose(4, 0, 1, 3, 2, 5).reshape(2, D)

    gate = gather_ring(gather_ring(gather_ring(gate, "x"), "y"), "z")
    up = gather_ring(gather_ring(gather_ring(up, "z"), "x"), "y")
    down = gather_ring(down_weight.astype(BF), "y").reshape(144, D)
    down_full = gather_ring(gather_ring(down, "z"), "x").reshape(HID, D)
    gate_full = feature_rows(gate.transpose(2, 0, 1, 3, 4), HID)
    up_full = feature_rows(up.transpose(1, 2, 0, 3, 4), HID)
    return in_full, out_full, gate_full, up_full, down_full, taps, gain_full


def rows_by_place(grad):
    return grad.reshape(4, 4, 2, 4, 8, grad.shape[1]).transpose(0, 1, 3, 2, 4, 5)


def scatter_a(blocks):
    return scatter_ring(scatter_ring(scatter_ring(blocks, "x", 0), "z", 0), "y", 0)


def scatter_b(blocks):
    return scatter_ring(scatter_ring(scatter_ring(blocks, "z", 1), "y", 1), "x", 0)


def scatter_c(blocks):
    return scatter_ring(scatter_ring(scatter_ring(blocks, "y", 2), "x", 0), "z", 0)


def shards(
    tokens,
    doc_lengths,
    cotangent,
    in_weight,
    in_first,
    in_second,
    out_weight,
    out_first,
    out_second,
    ffn_weight,
    ffn_first,
    ffn_second,
    down_weight,
    down_first,
    down_second,
    conv_weight,
    conv_first,
    conv_second,
    gains,
    gains_first,
    gains_second,
):
    core = lax.axis_index("core")
    in_full, out_full, gate_full, up_full, down_full, taps, gain_full = gather_weights(
        core, in_weight, out_weight, ffn_weight, down_weight, conv_weight, gains
    )
    other_tokens = swap(tokens)
    other_cot = swap(cotangent)
    other_lengths = swap(doc_lengths)
    values = jnp.concatenate(
        [pick(core, tokens, other_tokens), pick(core, other_tokens, tokens)], axis=0
    ).astype(F32)
    cot = jnp.concatenate([pick(core, cotangent, other_cot), pick(core, other_cot, cotangent)], axis=0)
    lengths = jnp.concatenate(
        [pick(core, doc_lengths, other_lengths), pick(core, other_lengths, doc_lengths)], axis=0
    )
    masks = tap_masks(lengths)
    gain_one = gain_full[0]
    gain_two = gain_full[1]

    def own_rows(value):
        return lax.dynamic_slice_in_dim(value, core * TOK, TOK, 0)

    def other_rows(value):
        return lax.dynamic_slice_in_dim(value, (1 - core) * TOK, TOK, 0)

    inverse_one = lax.rsqrt(jnp.mean(values * values, axis=1, keepdims=True) + eps_norm)
    normed_one = (values * inverse_one * gain_one).astype(BF)
    projected = dot(normed_one, in_full).reshape(2, TOK, 3 * CH)
    b_part = projected[..., :CH]
    c_part = projected[..., CH : 2 * CH]
    v_part = projected[..., 2 * CH :]
    mixed_in = b_part * v_part
    shifted = [delay_rows(mixed_in, offset) * masks[offset] for offset in range(3)]
    conv_out = taps[0] * shifted[0] + taps[1] * shifted[1] + taps[2] * shifted[2]
    gated = (c_part * conv_out).astype(BF).reshape(2 * TOK, CH)
    branch = dot(gated, out_full)
    middle = values + (branch + swap(branch))
    inverse_two = lax.rsqrt(jnp.mean(middle * middle, axis=1, keepdims=True) + eps_norm)
    normed_two = (middle * inverse_two * gain_two).astype(BF)
    gate_pre = dot(normed_two, gate_full)
    up_pre = dot(normed_two, up_full)
    sigmoid_gate = jax.nn.sigmoid(gate_pre)
    silu_gate = gate_pre * sigmoid_gate
    product = (silu_gate * up_pre).astype(BF)
    d_product = dot_nt(cot, down_full)
    d_gate = (d_product * up_pre * sigmoid_gate * (1.0 + gate_pre * (1.0 - sigmoid_gate))).astype(BF)
    d_up = (d_product * silu_gate).astype(BF)
    grad_down = dot_tn(product, cot).astype(BF)
    grad_gate = dot_tn(normed_two, d_gate).astype(BF)
    grad_up = dot_tn(normed_two, d_up).astype(BF)
    owned_down = scatter_a(grad_down.reshape(4, 4, 4, 36, D))
    owned_gate = scatter_b(rows_by_place(grad_gate))
    owned_up = scatter_c(rows_by_place(grad_up))

    ffn_out = dot(product, down_full)
    output = (own_rows(middle) + (own_rows(ffn_out) + swap(other_rows(ffn_out)))).astype(BF)

    d_normed_part = dot_nt(d_gate, gate_full) + dot_nt(d_up, up_full)
    d_normed_two = d_normed_part + swap(d_normed_part)
    grad_gain_two = jnp.sum(d_normed_two * middle * inverse_two, axis=0)
    scaled_two = d_normed_two * gain_two
    d_middle = (
        cot.astype(F32)
        + inverse_two * scaled_two
        - middle * inverse_two**3 * jnp.mean(scaled_two * middle, axis=1, keepdims=True)
    )
    d_middle_low = d_middle.astype(BF)
    grad_out = dot_tn(gated, d_middle_low).astype(BF)
    d_gated = dot_nt(d_middle_low, out_full).reshape(2, TOK, CH)
    d_c_part = d_gated * conv_out
    d_conv = d_gated * c_part
    grad_taps = jnp.stack([jnp.sum(d_conv * shifted[k], axis=(0, 1)) for k in range(3)])
    d_mixed = taps[0] * d_conv
    for offset in (1, 2):
        d_mixed = d_mixed + taps[offset] * advance_rows(d_conv * masks[offset], offset)
    d_proj = (
        jnp.concatenate([d_mixed * v_part, d_c_part, d_mixed * b_part], axis=-1)
        .astype(BF)
        .reshape(2 * TOK, 3 * CH)
    )
    grad_in = dot_tn(normed_one, d_proj).astype(BF)
    d_first_part = dot_nt(d_proj, in_full)
    d_normed_one = own_rows(d_first_part) + swap(other_rows(d_first_part))
    own_values = tokens.astype(F32)
    own_inverse = own_rows(inverse_one)
    grad_gain_one = jnp.sum(d_normed_one * own_values * own_inverse, axis=0)
    scaled_one = d_normed_one * gain_one
    tokens_grad = (
        own_rows(d_middle)
        + own_inverse * scaled_one
        - own_values * own_inverse**3 * jnp.mean(scaled_one * own_values, axis=1, keepdims=True)
    )

    in_places = [rows_by_place(grad_in[:, k * CH : (k + 1) * CH]) for k in range(3)]
    in_places = [part.reshape(4, 4, 4, 8 * 2, CH) for part in in_places]
    out_places = grad_out.reshape(4, 4, 4, 8, D)

    def conv_chain(part, out_part):
        both = part.reshape(4, 4, 4, 2, 8, CH).transpose(0, 1, 2, 4, 3, 5).reshape(4, 4, 4, 8, 2 * CH)
        return jnp.concatenate([both, out_part], axis=-1)

    owned_conv = [
        scatter_a(conv_chain(in_places[0], out_places[..., :384])),
        scatter_b(conv_chain(in_places[1], out_places[..., 384:768])),
        scatter_c(conv_chain(in_places[2], out_places[..., 768:])),
    ]
    gain_one_chip = grad_gain_one + swap(grad_gain_one)
    small = jnp.concatenate(
        [
            grad_taps,
            gain_one_chip.reshape(2, CH),
            grad_gain_two.reshape(2, CH),
            jnp.zeros((1, CH), F32),
        ],
        axis=0,
    )
    small = sum_all(small, ("x", "y", "z"))
    place = (lax.axis_index("x") * 4 + lax.axis_index("z")) * 4 + lax.axis_index("y")
    owned_taps = lax.dynamic_slice(small, (0, place * 8), (3, 8))
    gain_sums = jnp.stack([small[3:5].reshape(D), small[5:7].reshape(D)])
    mine = ((lax.axis_index("x") * 4 + lax.axis_index("z")) * 2 + core) * 4 + lax.axis_index("y")
    owned_gains = lax.dynamic_slice(gain_sums, (0, mine * 8), (2, 8))

    def rows_of(which):
        in_rows = [
            lax.dynamic_slice_in_dim(conv[:, : 2 * CH], which * CH, CH, 1) for conv in owned_conv
        ]
        ffn_rows = [
            lax.dynamic_index_in_dim(part, which, 0, keepdims=False)
            for part in (owned_gate, owned_up)
        ]
        return jnp.concatenate(in_rows + ffn_rows, axis=1)

    held = rows_of(core)
    came = swap(rows_of(1 - core))
    halves = (pick(core, held, came).astype(F32), pick(core, came, held).astype(F32))
    owned_in = join_cols([half[:, : 3 * CH] for half in halves], 3, 32)
    owned_ffn = join_cols([half[:, 3 * CH :] for half in halves], 2, 144)
    owned_out = jnp.concatenate([conv[:, 2 * CH :] for conv in owned_conv], axis=1).astype(F32)
    owned = (owned_in, owned_out, owned_ffn, owned_down.astype(F32), owned_taps, owned_gains)

    local_squares = F32(0.0)
    for grad in owned:
        local_squares = local_squares + jnp.sum(grad * grad)
    squares = sum_all(local_squares.reshape(1, 1), ("core", "x", "y", "z"))[0, 0]
    grad_norm = jnp.sqrt(squares)
    factor = jnp.minimum(1.0, clip_level / grad_norm)
    states = (
        (in_weight, in_first, in_second),
        (out_weight, out_first, out_second),
        (ffn_weight, ffn_first, ffn_second),
        (down_weight, down_first, down_second),
        (conv_weight, conv_first, conv_second),
        (gains, gains_first, gains_second),
    )
    results = []
    for index in range(6):
        rate = rate_matrix if index < 4 else rate_vector
        decay = decay_matrix if index < 4 else 0.0
        weight, first, second = states[index]
        results.extend(adam_step(weight, first, second, owned[index] * factor, rate, decay))
    return (output, tokens_grad, grad_norm, *results)


def solution(mesh):
    chips = Mesh(mesh.devices.reshape(4, 4, 2, 4), AXES)
    rows = P(AXES, None)
    columns = P(None, AXES)
    return jax.shard_map(
        shards,
        mesh=chips,
        in_specs=(rows,) * 15 + (columns,) * 6,
        out_specs=(rows, rows, P()) + (rows,) * 12 + (columns,) * 6,
        check_vma=False,
    )
```

time: 1590 us -> 607 us (0.38)
  blocking collectives: 616 us -> 0 us
  waiting for transfers between devices: 754 us -> 233 us
  local copies, waits for them, and re-layouts: 40.2 us -> 126 us
  starting transfers between devices: 27.3 us -> 106 us
  matrix products: 92.2 us -> 59.5 us
  other arithmetic: 33.3 us -> 57.8 us
    reduce_scatter x3 -> x0, waiting for transfers between devices: 593 us -> none  [the longest x1 282 us: reduce_grads(): lax.psum_scatter(grads[2], ('group', 'shard'), scatter_dimension=0, tiled...]
    unnamed x2 -> x0, blocking collectives: 447 us -> none
    ppermute x0 -> x138, waiting for transfers between devices: none -> 233 us  [the longest x108 216 us: hop(): return lax.ppermute(value, names, ring_pairs(axis))]
    all_gather x4 -> x0, waiting for transfers between devices: 158 us -> none  [the longest x1 71.8 us: gather_weights(): lax.all_gather(pieces[2], ('group', 'shard'), axis=0, tiled=True)]
    all_gather x2 -> x0, blocking collectives: 106 us -> none  [the longest x1 53.4 us: gather_weights(): lax.all_gather(pieces[4], ('group', 'shard'), axis=1, tiled=True)]
    ppermute x0 -> x138, starting transfers between devices: none -> 106 us  [the longest x108 57.8 us: hop(): return lax.ppermute(value, names, ring_pairs(axis))]
    psum x1 -> x0, blocking collectives: 62.7 us -> none  [shards(): squares = lax.psum(local_squares, ('group', 'shard'))]
    dynamic_update_slice x0 -> x66, local copies, waits for them, and re-layouts: none -> 37.4 us  [gather_ring(): lax.dynamic_update_slice(stacked, block[None], (index,) + (0,) * block.ndim)]
  transfers between devices with their start and end apart: 20 -> 138, of which waited for: 8 -> 73; matrix products, arithmetic and copies ran while one was open for 30% -> 27% of each run, Pallas kernels for 0% -> 0%
where the time goes in v1:
time: 607 us; the launch traced here: 596 us
  waiting for transfers between devices  233 us (38%)
  local copies, waits for them, and re-layouts  126 us (21%)
  starting transfers between devices  106 us (17%)
  matrix products  59.5 us (10%)
  other arithmetic  57.8 us (10%)
  between operations  14.8 us (2%)
    ppermute x108, waiting for transfers between devices, hop(): return lax.ppermute(value, names, ring_pairs(axis))  216 us
    ppermute x108, starting transfers between devices, hop(): return lax.ppermute(value, names, ring_pairs(axis))  57.8 us
    ppermute x18, starting transfers between devices, sum_all(): lax.ppermute(value, name, [(i, (i + shift) % 4) for i in range(4)])  39.7 us
    dynamic_update_slice x66, local copies, waits for them, and re-layouts, gather_ring(): lax.dynamic_update_slice(stacked, block[None], (index,) + (0,) * block.ndim)  37.4 us
    convert_element_type x53, other arithmetic, scatter_ring(): moving = (arrived.astype(F32) + own(step % 4).astype(F32)).astype(BF)  23.3 us
    dot_general x5, matrix products, dot(): return jnp.dot(left, right, preferred_element_type=F32)  22.9 us
    reshape x5, local copies, waits for them, and re-layouts, feature_rows(): split = value.reshape(4, 4, 4, 8, 2, width).transpose(0, 1, 4, 2, 3, 5)  22.6 us
    dot_general x5, matrix products, dot_nt(): lax.dot_general(left, right, (((1,), (1,)), ((), ())), preferred_element_...  19.7 us
  transfers between devices with their start and end apart: 138, of which 73 were waited for; matrix products, arithmetic and copies ran while one was open for 27% of the time, Pallas kernels for 0%

profile of v1, /device:TPU:0, one launch (start us, length us, event | category | flops | bytes accessed | tf_op | source)
XLA Modules:
  0.0 596.3 jit_solution(11309227014151519336)
XLA Ops:
  15.0 3.3 collective-permute-done.12
  19.8 3.5 collective-permute-done.21
  25.3 3.1 collective-permute-done.3
  28.7 4.7 collective-permute-done.13
  33.7 4.7 collective-permute-done.22
  39.1 4.3 collective-permute-done.4
  43.5 5.0 collective-permute-done.14
  49.1 4.4 collective-permute-done.23
  53.6 4.9 collective-permute-done.5
  61.0 3.2 collective-permute-done.52
  65.2 4.8 collective-permute-done.42
  71.6 4.2 collective-permute-done.33
  76.8 4.7 collective-permute-done.6
  82.2 3.4 collective-permute-done.43
  91.4 3.5 collective-permute-done.25
  97.7 5.1 collective-permute-done.17
  104.1 4.4 collective-permute-done.26
  108.8 5.5 collective-permute-done.8
  162.7 4.5 collective-permute-done.20
  191.2 5.1 fusion.14
  198.9 3.4 multiply_convert_fusion.7
  214.6 7.6 %collective-permute-done.57 = bf16[4,144,1024]{2,1,0:T(8,128)(2,1)S(1)} collective-permute-done((bf16[4,144,1024]{2,1,0:T(8,128)(2,1)}, bf16[4,144,1024]{2,1,0:T(8,128)(2,1)S(1)}, u32[]{:S(2)}, u32[]{:S(2)}) %collective-permute-start.57) | collective-permute-done | bytes 1179680 | tf_op jit(solution)/shard_map/ppermute | solution.py:55
  236.1 3.5 collective-permute-done.58
  244.3 7.4 %reshape.433 = bf16[4,4,4,8,2,2304]{5,4,3,2,1,0:T(2,128)(2,1)} reshape(bf16[4,4,4,8,4608]{4,3,2,1,0:T(8,128)(2,1)} %bitcast.95) | data formatting | bytes 9437184 | tf_op jit(solution)/shard_map/reshape | solution.py:184
  251.7 5.4 copy.294
  259.4 7.3 %reshape.511 = bf16[4,4,4,8,2,2304]{5,4,3,1,0,2:T(2,128)(2,1)} reshape(bf16[4,4,4,8,4608]{4,3,1,0,2:T(8,128)(2,1)} %bitcast.76) | data formatting | bytes 9437184 | tf_op jit(solution)/shard_map/reshape | solution.py:184
  266.7 3.2 copy.290
  269.9 5.0 fusion.156
  274.9 4.3 fusion.155
  279.1 9.5 %multiply_convert_fusion = (bf16[512,2304]{1,0:T(8,128)(2,1)}, bf16[512,2304]{1,0:T(8,128)(2,1)S(1)}, bf16[512,2304]{1,0:T(8,128)(2,1)}) fusion(f32[512,2304]{1,0:T(8,128)} %fusion.155, f32[512,2304]{1,0:T(8,128)S(1)} %fusion.156, bf16[2304,1024]{1,0:T(8,128)(2,1)} %bitcast.109, bf16[256,1024]{1,0:T(8,128)(2,1)S(1)} %copy-done.26, ...), kind=kOutput, calls=%fused_computation.3 | convolution fusion | flops 2435710976 | bytes 22282240 | tf_op jit(solution)/shard_map/dot_general | solution.py:38
  288.6 6.9 %convolution_convert_fusion = bf16[2304,1024]{1,0:T(8,128)(2,1)} fusion(bf16[512,2304]{1,0:T(8,128)(2,1)} %get-tuple-element.67, bf16[256,1024]{1,0:T(8,128)(2,1)S(1)} %copy-done.26, bf16[256,1024]{1,0:T(8,128)(2,1)S(1)} %copy-done.24), kind=kOutput, calls=%fused_computation | convolution fusion | flops 2420375552 | bytes 8126464 | tf_op jit(solution)/shard_map/dot_general | solution.py:34
  295.5 6.5 %fusion.157 = f32[512,1024]{1,0:T(8,128)} fusion(bf16[512,2304]{1,0:T(8,128)(2,1)S(1)} %copy-done.88, bf16[2304,1024]{1,0:T(8,128)(2,1)} %bitcast.109), kind=kOutput, calls=%fused_computation.464 | convolution fusion | flops 2415919104 | bytes 9175040 | tf_op jit(solution)/shard_map/dot_general | solution.py:30
  304.6 4.5 convolution_convert_fusion.1
  309.2 4.0 convolution_add_fusion
  313.2 7.2 %reshape.450 = bf16[4,4,4,36,1024]{4,3,2,1,0:T(8,128)(2,1)} reshape(bf16[2304,1024]{1,0:T(8,128)(2,1)} %convolution_convert_fusion) | data formatting | bytes 9437184 | tf_op jit(solution)/shard_map/reshape | solution.py:295
  325.2 2.9 convolution_convert_fusion.2
  332.3 8.0 %collective-permute-done.109 = bf16[4,4,36,1024]{3,1,2,0:T(4,128)(2,1)S(1)} collective-permute-done((bf16[4,4,36,1024]{3,1,2,0:T(4,128)(2,1)S(1)}, bf16[4,4,36,1024]{3,1,2,0:T(4,128)(2,1)S(1)}, u32[]{:S(2)}, u32[]{:S(2)}) %collective-permute-start.109) | collective-permute-done | bytes 1179680 | tf_op jit(solution)/shard_map/ppermute | solution.py:55
  374.2 2.9 fusion.5
  378.8 2.9 fusion.8
  385.6 4.7 collective-permute-done.82
  393.0 5.6 collective-permute-done.64
  401.9 4.1 collective-permute-start.118
  418.0 3.6 collective-permute-done.65
  421.6 3.2 collective-permute-start.124
  424.9 5.0 collective-permute-done.122
  438.7 4.0 collective-permute-done.85
  444.0 4.7 collective-permute-done.86
  448.8 5.7 collective-permute-done.66
  454.4 5.0 collective-permute-done.87
  459.5 5.8 collective-permute-done.88
  465.7 4.9 collective-permute-done.89
  471.4 5.0 collective-permute-done.68
  477.7 3.8 collective-permute-done.69
  482.6 4.0 collective-permute-done.70
  487.6 4.1 collective-permute-done.71
  498.3 4.7 collective-permute-done.112
  506.4 5.1 collective-permute-done.113
  514.5 5.5 collective-permute-done.114
  528.2 3.3 collective-permute-done.116
  534.3 5.2 collective-permute-done.98
  550.7 4.5 collective-permute-start.131
  563.5 4.5 collective-permute-start.134
  569.3 3.9 collective-permute-done.132
  576.3 4.5 collective-permute-start.137
  (728 shorter events, 278.4 us)
Async XLA Ops:
  4.3 112.0 %collective-permute-start = (bf16[256,1024]{1,0:T(8,128)(2,1)S(1)}, bf16[256,1024]{1,0:T(8,128)(2,1)}, u32[]{:S(2)}, u32[]{:S(2)}) collective-permute-start(bf16[256,1024]{1,0:T(8,128)(2,1)S(1)} %copy-done.7), channel_id=1, source_target_pairs={{0,4},{4,0},{1,5},{5,1},{2,6},{6,2},{3,7},{7,3},{8,12},{12,8},{9,1... | collective-permute-start | bytes 1572872 | tf_op jit(solution)/shard_map/ppermute | solution.py:59
  7.2 111.3 %collective-permute-start.60 = (bf16[256,1024]{1,0:T(8,128)(2,1)}, bf16[256,1024]{1,0:T(8,128)(2,1)}, u32[]{:S(2)}, u32[]{:S(2)}) collective-permute-start(bf16[256,1024]{1,0:T(8,128)(2,1)} %param.23), channel_id=1, source_target_pairs={{0,4},{4,0},{1,5},{5,1},{2,6},{6,2},{3,7},{7,3},{8,12},{12,8},{9,1... | collective-permute-start | bytes 1572872 | tf_op jit(solution)/shard_map/ppermute | solution.py:59
  10.8 32.7 %collective-permute-start.51 = (bf16[36,1024]{1,0:T(8,128)(2,1)S(1)}, bf16[36,1024]{1,0:T(8,128)(2,1)S(1)}, u32[]{:S(2)}, u32[]{:S(2)}) collective-permute-start(bf16[36,1024]{1,0:T(8,128)(2,1)S(1)} %collective-permute-done.50), channel_id=1, source_target_pairs={{0,1},{4,7},{1,2},{5,4},{2,3},{6,5},{3,0},{7,6},{8,9},{12,15},{9,1... | collective-permute-start | bytes 221192 | tf_op jit(solution)/shard_map/ppermute | solution.py:55
  11.2 48.7 %collective-permute-start.41 = (bf16[8,4608]{1,0:T(8,128)(2,1)S(1)}, bf16[8,4608]{1,0:T(8,128)(2,1)}, u32[]{:S(2)}, u32[]{:S(2)}) collective-permute-start(bf16[8,4608]{1,0:T(8,128)(2,1)S(1)} %pad_maximum_fusion.13), channel_id=1, source_target_pairs={{0,8},{4,28},{8,16},{12,4},{16,24},{20,12},{24,0},{28,20},{1,9},{5... | collective-permute-start | bytes 221192 | tf_op jit(solution)/shard_map/ppermute | solution.py:55
  43.4 17.5 %collective-permute-start.32 = (bf16[8,4608]{1,0:T(8,128)(2,1)S(1)}, bf16[8,4608]{1,0:T(8,128)(2,1)S(1)}, u32[]{:S(2)}, u32[]{:S(2)}) collective-permute-start(bf16[8,4608]{1,0:T(8,128)(2,1)S(1)} %pad_maximum_fusion.12), channel_id=1, source_target_pairs={{0,32},{4,100},{32,64},{36,4},{64,96},{68,36},{96,0},{100,68},{1,3... | collective-permute-start | bytes 221192 | tf_op jit(solution)/shard_map/ppermute | solution.py:55
  60.0 16.5 %collective-permute-start.15 = (bf16[4,8,1408]{2,1,0:T(8,128)(2,1)S(1)}, bf16[4,8,1408]{2,1,0:T(8,128)(2,1)S(1)}, u32[]{:S(2)}, u32[]{:S(2)}) collective-permute-start(bf16[4,8,1408]{2,1,0:T(8,128)(2,1)S(1)} %constant_dynamic-update-slice_fusion.5), channel_id=1, source_target_pairs={{0,8},{4,28},{8,16},{12,4},{16,24},{20,12},{24,0},{28,20},{1,9},{5... | collective-permute-start | bytes 270344 | tf_op jit(solution)/shard_map/ppermute | solution.py:55
  60.9 15.9 %collective-permute-start.24 = (bf16[4,8,1408]{2,1,0:T(8,128)(2,1)S(1)}, bf16[4,8,1408]{2,1,0:T(8,128)(2,1)S(1)}, u32[]{:S(2)}, u32[]{:S(2)}) collective-permute-start(bf16[4,8,1408]{2,1,0:T(8,128)(2,1)S(1)} %constant_dynamic-update-slice_fusion.1), channel_id=1, source_target_pairs={{0,1},{4,7},{1,2},{5,4},{2,3},{6,5},{3,0},{7,6},{8,9},{12,15},{9,1... | collective-permute-start | bytes 270344 | tf_op jit(solution)/shard_map/ppermute | solution.py:55
  76.5 39.7 %collective-permute-start.53 = (bf16[144,1024]{1,0:T(8,128)(2,1)}, bf16[144,1024]{1,0:T(8,128)(2,1)S(1)}, u32[]{:S(2)}, u32[]{:S(2)}) collective-permute-start(bf16[144,1024]{1,0:T(8,128)(2,1)} %reshape.435), channel_id=1, source_target_pairs={{0,8},{4,28},{8,16},{12,4},{16,24},{20,12},{24,0},{28,20},{1,9},{5... | collective-permute-start | bytes 884744 | tf_op jit(solution)/shard_map/ppermute | solution.py:55
  76.7 8.9 %collective-permute-start.43 = (bf16[8,4608]{1,0:T(8,128)(2,1)}, bf16[8,4608]{1,0:T(8,128)(2,1)S(1)}, u32[]{:S(2)}, u32[]{:S(2)}) collective-permute-start(bf16[8,4608]{1,0:T(8,128)(2,1)} %collective-permute-done.42), channel_id=1, source_target_pairs={{0,8},{4,28},{8,16},{12,4},{16,24},{20,12},{24,0},{28,20},{1,9},{5... | collective-permute-start | bytes 221192 | tf_op jit(solution)/shard_map/ppermute | solution.py:55
  94.8 26.5 %collective-permute-start.44 = (bf16[4,8,4608]{2,1,0:T(8,128)(2,1)S(1)}, bf16[4,8,4608]{2,1,0:T(8,128)(2,1)S(1)}, u32[]{:S(2)}, u32[]{:S(2)}) collective-permute-start(bf16[4,8,4608]{2,1,0:T(8,128)(2,1)S(1)} %copy-done.40), channel_id=1, source_target_pairs={{0,32},{4,100},{32,64},{36,4},{64,96},{68,36},{96,0},{100,68},{1,3... | collective-permute-start | bytes 884744 | tf_op jit(solution)/shard_map/ppermute | solution.py:55
  114.3 8.8 %collective-permute-start.35 = (bf16[4,8,4608]{2,1,0:T(8,128)(2,1)S(1)}, bf16[4,8,4608]{2,1,0:T(8,128)(2,1)S(1)}, u32[]{:S(2)}, u32[]{:S(2)}) collective-permute-start(bf16[4,8,4608]{2,1,0:T(8,128)(2,1)S(1)} %bitcast_dynamic-update-slice_fusion.51), channel_id=1, source_target_pairs={{0,1},{4,7},{1,2},{5,4},{2,3},{6,5},{3,0},{7,6},{8,9},{12,15},{9,1... | collective-permute-start | bytes 884744 | tf_op jit(solution)/shard_map/ppermute | solution.py:55
  116.3 10.1 %collective-permute-start.27 = (bf16[4,4,8,1408]{3,2,1,0:T(8,128)(2,1)S(1)}, bf16[4,4,8,1408]{3,2,1,0:T(8,128)(2,1)S(1)}, u32[]{:S(2)}, u32[]{:S(2)}) collective-permute-start(bf16[4,4,8,1408]{3,2,1,0:T(8,128)(2,1)S(1)} %copy-done.34), channel_id=1, source_target_pairs={{0,8},{4,28},{8,16},{12,4},{16,24},{20,12},{24,0},{28,20},{1,9},{5... | collective-permute-start | bytes 1081352 | tf_op jit(solution)/shard_map/ppermute | solution.py:55
  118.5 10.3 %collective-permute-start.9 = (bf16[4,4,8,1408]{3,2,1,0:T(8,128)(2,1)}, bf16[4,4,8,1408]{3,2,1,0:T(8,128)(2,1)S(1)}, u32[]{:S(2)}, u32[]{:S(2)}) collective-permute-start(bf16[4,4,8,1408]{3,2,1,0:T(8,128)(2,1)} %bitcast_dynamic-update-slice_fusion.39), channel_id=1, source_target_pairs={{0,1},{4,7},{1,2},{5,4},{2,3},{6,5},{3,0},{7,6},{8,9},{12,15},{9,1... | collective-permute-start | bytes 1081352 | tf_op jit(solution)/shard_map/ppermute | solution.py:55
  121.4 9.9 %collective-permute-start.54 = (bf16[144,1024]{1,0:T(8,128)(2,1)S(1)}, bf16[144,1024]{1,0:T(8,128)(2,1)S(1)}, u32[]{:S(2)}, u32[]{:S(2)}) collective-permute-start(bf16[144,1024]{1,0:T(8,128)(2,1)S(1)} %collective-permute-done.53), channel_id=1, source_target_pairs={{0,8},{4,28},{8,16},{12,4},{16,24},{20,12},{24,0},{28,20},{1,9},{5... | collective-permute-start | bytes 884744 | tf_op jit(solution)/shard_map/ppermute | solution.py:55
  123.1 9.4 %collective-permute-start.45 = (bf16[4,8,4608]{2,1,0:T(8,128)(2,1)S(1)}, bf16[4,8,4608]{2,1,0:T(8,128)(2,1)S(1)}, u32[]{:S(2)}, u32[]{:S(2)}) collective-permute-start(bf16[4,8,4608]{2,1,0:T(8,128)(2,1)S(1)} %collective-permute-done.44), channel_id=1, source_target_pairs={{0,32},{4,100},{32,64},{36,4},{64,96},{68,36},{96,0},{100,68},{1,3... | collective-permute-start | bytes 884744 | tf_op jit(solution)/shard_map/ppermute | solution.py:55
  124.9 10.1 %collective-permute-start.36 = (bf16[4,8,4608]{2,1,0:T(8,128)(2,1)S(1)}, bf16[4,8,4608]{2,1,0:T(8,128)(2,1)S(1)}, u32[]{:S(2)}, u32[]{:S(2)}) collective-permute-start(bf16[4,8,4608]{2,1,0:T(8,128)(2,1)S(1)} %collective-permute-done.35), channel_id=1, source_target_pairs={{0,1},{4,7},{1,2},{5,4},{2,3},{6,5},{3,0},{7,6},{8,9},{12,15},{9,1... | collective-permute-start | bytes 884744 | tf_op jit(solution)/shard_map/ppermute | solution.py:55
  126.4 19.4 %collective-permute-start.19 = (bf16[4,4,8,1408]{3,2,1,0:T(8,128)(2,1)S(1)}, bf16[4,4,8,1408]{3,2,1,0:T(8,128)(2,1)S(1)}, u32[]{:S(2)}, u32[]{:S(2)}) collective-permute-start(bf16[4,4,8,1408]{3,2,1,0:T(8,128)(2,1)S(1)} %collective-permute-done.18), channel_id=1, source_target_pairs={{0,32},{4,100},{32,64},{36,4},{64,96},{68,36},{96,0},{100,68},{1,3... | collective-permute-start | bytes 1081352 | tf_op jit(solution)/shard_map/ppermute | solution.py:55
  128.7 19.5 %collective-permute-start.28 = (bf16[4,4,8,1408]{3,2,1,0:T(8,128)(2,1)S(1)}, bf16[4,4,8,1408]{3,2,1,0:T(8,128)(2,1)S(1)}, u32[]{:S(2)}, u32[]{:S(2)}) collective-permute-start(bf16[4,4,8,1408]{3,2,1,0:T(8,128)(2,1)S(1)} %collective-permute-done.27), channel_id=1, source_target_pairs={{0,8},{4,28},{8,16},{12,4},{16,24},{20,12},{24,0},{28,20},{1,9},{5... | collective-permute-start | bytes 1081352 | tf_op jit(solution)/shard_map/ppermute | solution.py:55
  131.3 17.1 %collective-permute-start.10 = (bf16[4,4,8,1408]{3,2,1,0:T(8,128)(2,1)S(1)}, bf16[4,4,8,1408]{3,2,1,0:T(8,128)(2,1)S(1)}, u32[]{:S(2)}, u32[]{:S(2)}) collective-permute-start(bf16[4,4,8,1408]{3,2,1,0:T(8,128)(2,1)S(1)} %collective-permute-done.9), channel_id=1, source_target_pairs={{0,1},{4,7},{1,2},{5,4},{2,3},{6,5},{3,0},{7,6},{8,9},{12,15},{9,1... | collective-permute-start | bytes 1081352 | tf_op jit(solution)/shard_map/ppermute | solution.py:55
  135.0 14.7 %collective-permute-start.46 = (bf16[4,8,4608]{2,1,0:T(8,128)(2,1)S(1)}, bf16[4,8,4608]{2,1,0:T(8,128)(2,1)S(1)}, u32[]{:S(2)}, u32[]{:S(2)}) collective-permute-start(bf16[4,8,4608]{2,1,0:T(8,128)(2,1)S(1)} %collective-permute-done.45), channel_id=1, source_target_pairs={{0,32},{4,100},{32,64},{36,4},{64,96},{68,36},{96,0},{100,68},{1,3... | collective-permute-start | bytes 884744 | tf_op jit(solution)/shard_map/ppermute | solution.py:55
  140.6 15.6 %collective-permute-start.37 = (bf16[4,8,4608]{2,1,0:T(8,128)(2,1)S(1)}, bf16[4,8,4608]{2,1,0:T(8,128)(2,1)S(1)}, u32[]{:S(2)}, u32[]{:S(2)}) collective-permute-start(bf16[4,8,4608]{2,1,0:T(8,128)(2,1)S(1)} %collective-permute-done.36), channel_id=1, source_target_pairs={{0,1},{4,7},{1,2},{5,4},{2,3},{6,5},{3,0},{7,6},{8,9},{12,15},{9,1... | collective-permute-start | bytes 884744 | tf_op jit(solution)/shard_map/ppermute | solution.py:55
  145.8 58.6 %collective-permute-start.56 = (bf16[4,144,1024]{2,1,0:T(8,128)(2,1)S(1)}, bf16[4,144,1024]{2,1,0:T(8,128)(2,1)}, u32[]{:S(2)}, u32[]{:S(2)}) collective-permute-start(bf16[4,144,1024]{2,1,0:T(8,128)(2,1)S(1)} %bitcast_dynamic-update-slice_fusion.20), channel_id=1, source_target_pairs={{0,32},{4,100},{32,64},{36,4},{64,96},{68,36},{96,0},{100,68},{1,3... | collective-permute-start | bytes 3538952 | tf_op jit(solution)/shard_map/ppermute | solution.py:55
  148.3 18.8 %collective-permute-start.20 = (bf16[4,4,8,1408]{3,2,1,0:T(8,128)(2,1)S(1)}, bf16[4,4,8,1408]{3,2,1,0:T(8,128)(2,1)S(1)}, u32[]{:S(2)}, u32[]{:S(2)}) collective-permute-start(bf16[4,4,8,1408]{3,2,1,0:T(8,128)(2,1)S(1)} %collective-permute-done.19), channel_id=1, source_target_pairs={{0,32},{4,100},{32,64},{36,4},{64,96},{68,36},{96,0},{100,68},{1,3... | collective-permute-start | bytes 1081352 | tf_op jit(solution)/shard_map/ppermute | solution.py:55
  148.4 21.9 %collective-permute-start.29 = (bf16[4,4,8,1408]{3,2,1,0:T(8,128)(2,1)S(1)}, bf16[4,4,8,1408]{3,2,1,0:T(8,128)(2,1)S(1)}, u32[]{:S(2)}, u32[]{:S(2)}) collective-permute-start(bf16[4,4,8,1408]{3,2,1,0:T(8,128)(2,1)S(1)} %collective-permute-done.28), channel_id=1, source_target_pairs={{0,8},{4,28},{8,16},{12,4},{16,24},{20,12},{24,0},{28,20},{1,9},{5... | collective-permute-start | bytes 1081352 | tf_op jit(solution)/shard_map/ppermute | solution.py:55
  149.7 22.5 %collective-permute-start.11 = (bf16[4,4,8,1408]{3,2,1,0:T(8,128)(2,1)S(1)}, bf16[4,4,8,1408]{3,2,1,0:T(8,128)(2,1)S(1)}, u32[]{:S(2)}, u32[]{:S(2)}) collective-permute-start(bf16[4,4,8,1408]{3,2,1,0:T(8,128)(2,1)S(1)} %collective-permute-done.10), channel_id=1, source_target_pairs={{0,1},{4,7},{1,2},{5,4},{2,3},{6,5},{3,0},{7,6},{8,9},{12,15},{9,1... | collective-permute-start | bytes 1081352 | tf_op jit(solution)/shard_map/ppermute | solution.py:55
  156.2 51.9 %collective-permute-start.47 = (bf16[4,4,8,4608]{3,2,1,0:T(8,128)(2,1)}, bf16[4,4,8,4608]{3,2,1,0:T(8,128)(2,1)}, u32[]{:S(2)}, u32[]{:S(2)}) collective-permute-start(bf16[4,4,8,4608]{3,2,1,0:T(8,128)(2,1)} %bitcast_dynamic-update-slice_fusion.23), channel_id=1, source_target_pairs={{0,1},{4,7},{1,2},{5,4},{2,3},{6,5},{3,0},{7,6},{8,9},{12,15},{9,1... | collective-permute-start | bytes 3538952 | tf_op jit(solution)/shard_map/ppermute | solution.py:55
  167.1 43.7 %collective-permute-start.38 = (bf16[4,4,8,4608]{3,2,1,0:T(8,128)(2,1)}, bf16[4,4,8,4608]{3,2,1,0:T(8,128)(2,1)}, u32[]{:S(2)}, u32[]{:S(2)}) collective-permute-start(bf16[4,4,8,4608]{3,2,1,0:T(8,128)(2,1)} %bitcast_dynamic-update-slice_fusion.27), channel_id=1, source_target_pairs={{0,8},{4,28},{8,16},{12,4},{16,24},{20,12},{24,0},{28,20},{1,9},{5... | collective-permute-start | bytes 3538952 | tf_op jit(solution)/shard_map/ppermute | solution.py:55
  204.3 27.9 %collective-permute-start.31 = (f32[512,1024]{1,0:T(8,128)}, f32[512,1024]{1,0:T(8,128)}, u32[]{:S(2)}, u32[]{:S(2)}) collective-permute-start(f32[512,1024]{1,0:T(8,128)} %fusion.154), channel_id=1, source_target_pairs={{0,4},{4,0},{1,5},{5,1},{2,6},{6,2},{3,7},{7,3},{8,12},{12,8},{9,1... | collective-permute-start | bytes 6291464 | tf_op jit(solution)/shard_map/ppermute | solution.py:59
  204.5 17.7 %collective-permute-start.57 = (bf16[4,144,1024]{2,1,0:T(8,128)(2,1)}, bf16[4,144,1024]{2,1,0:T(8,128)(2,1)S(1)}, u32[]{:S(2)}, u32[]{:S(2)}) collective-permute-start(bf16[4,144,1024]{2,1,0:T(8,128)(2,1)} %collective-permute-done.56), channel_id=1, source_target_pairs={{0,32},{4,100},{32,64},{36,4},{64,96},{68,36},{96,0},{100,68},{1,3... | collective-permute-start | bytes 3538952 | tf_op jit(solution)/shard_map/ppermute | solution.py:55
  208.1 17.6 %collective-permute-start.48 = (bf16[4,4,8,4608]{3,2,1,0:T(8,128)(2,1)}, bf16[4,4,8,4608]{3,2,1,0:T(8,128)(2,1)S(1)}, u32[]{:S(2)}, u32[]{:S(2)}) collective-permute-start(bf16[4,4,8,4608]{3,2,1,0:T(8,128)(2,1)} %collective-permute-done.47), channel_id=1, source_target_pairs={{0,1},{4,7},{1,2},{5,4},{2,3},{6,5},{3,0},{7,6},{8,9},{12,15},{9,1... | collective-permute-start | bytes 3538952 | tf_op jit(solution)/shard_map/ppermute | solution.py:55
  210.9 17.7 %collective-permute-start.39 = (bf16[4,4,8,4608]{3,2,1,0:T(8,128)(2,1)}, bf16[4,4,8,4608]{3,2,1,0:T(8,128)(2,1)}, u32[]{:S(2)}, u32[]{:S(2)}) collective-permute-start(bf16[4,4,8,4608]{3,2,1,0:T(8,128)(2,1)} %collective-permute-done.38), channel_id=1, source_target_pairs={{0,8},{4,28},{8,16},{12,4},{16,24},{20,12},{24,0},{28,20},{1,9},{5... | collective-permute-start | bytes 3538952 | tf_op jit(solution)/shard_map/ppermute | solution.py:55
  222.2 17.4 %collective-permute-start.58 = (bf16[4,144,1024]{2,1,0:T(8,128)(2,1)S(1)}, bf16[4,144,1024]{2,1,0:T(8,128)(2,1)S(1)}, u32[]{:S(2)}, u32[]{:S(2)}) collective-permute-start(bf16[4,144,1024]{2,1,0:T(8,128)(2,1)S(1)} %collective-permute-done.57), channel_id=1, source_target_pairs={{0,32},{4,100},{32,64},{36,4},{64,96},{68,36},{96,0},{100,68},{1,3... | collective-permute-start | bytes 3538952 | tf_op jit(solution)/shard_map/ppermute | solution.py:55
  225.7 17.4 %collective-permute-start.49 = (bf16[4,4,8,4608]{3,2,1,0:T(8,128)(2,1)S(1)}, bf16[4,4,8,4608]{3,2,1,0:T(8,128)(2,1)S(1)}, u32[]{:S(2)}, u32[]{:S(2)}) collective-permute-start(bf16[4,4,8,4608]{3,2,1,0:T(8,128)(2,1)S(1)} %collective-permute-done.48), channel_id=1, source_target_pairs={{0,1},{4,7},{1,2},{5,4},{2,3},{6,5},{3,0},{7,6},{8,9},{12,15},{9,1... | collective-permute-start | bytes 3538952 | tf_op jit(solution)/shard_map/ppermute | solution.py:55
  228.6 28.5 %collective-permute-start.40 = (bf16[4,4,8,4608]{3,2,1,0:T(8,128)(2,1)}, bf16[4,4,8,4608]{3,2,1,0:T(8,128)(2,1)}, u32[]{:S(2)}, u32[]{:S(2)}) collective-permute-start(bf16[4,4,8,4608]{3,2,1,0:T(8,128)(2,1)} %collective-permute-done.39), channel_id=1, source_target_pairs={{0,8},{4,28},{8,16},{12,4},{16,24},{20,12},{24,0},{28,20},{1,9},{5... | collective-permute-start | bytes 3538952 | tf_op jit(solution)/shard_map/ppermute | solution.py:55
  322.9 17.5 %collective-permute-start.109 = (bf16[4,4,36,1024]{3,1,2,0:T(4,128)(2,1)S(1)}, bf16[4,4,36,1024]{3,1,2,0:T(4,128)(2,1)S(1)}, u32[]{:S(2)}, u32[]{:S(2)}) collective-permute-start(bf16[4,4,36,1024]{3,1,2,0:T(4,128)(2,1)S(1)} %bitcast.628), channel_id=1, source_target_pairs={{0,32},{4,100},{32,64},{36,4},{64,96},{68,36},{96,0},{100,68},{1,3... | collective-permute-start | bytes 3538952 | tf_op jit(solution)/shard_map/ppermute | solution.py:55
  324.7 19.4 %collective-permute-start.99 = (bf16[4,4,2,8,2304]{4,3,2,1,0:T(8,128)(2,1)S(1)}, bf16[4,4,2,8,2304]{4,3,2,1,0:T(8,128)(2,1)S(1)}, u32[]{:S(2)}, u32[]{:S(2)}) collective-permute-start(bf16[4,4,2,8,2304]{4,3,2,1,0:T(8,128)(2,1)S(1)} %dynamic-slice_bitcast_fusion), channel_id=1, source_target_pairs={{0,1},{4,7},{1,2},{5,4},{2,3},{6,5},{3,0},{7,6},{8,9},{12,15},{9,1... | collective-permute-start | bytes 3538952 | tf_op jit(solution)/shard_map/ppermute | solution.py:55
  328.1 20.7 %collective-permute-start.61 = (f32[512,1024]{1,0:T(8,128)S(1)}, f32[512,1024]{1,0:T(8,128)S(1)}, u32[]{:S(2)}, u32[]{:S(2)}) collective-permute-start(f32[512,1024]{1,0:T(8,128)S(1)} %copy-done.5), channel_id=1, source_target_pairs={{0,4},{4,0},{1,5},{5,1},{2,6},{6,2},{3,7},{7,3},{8,12},{12,8},{9,1... | collective-permute-start | bytes 6291464 | tf_op jit(solution)/shard_map/ppermute | solution.py:59
  328.6 17.5 %collective-permute-start.90 = (bf16[4,4,2,8,2304]{4,3,1,2,0:T(8,128)(2,1)S(1)}, bf16[4,4,2,8,2304]{4,3,1,2,0:T(8,128)(2,1)S(1)}, u32[]{:S(2)}, u32[]{:S(2)}) collective-permute-start(bf16[4,4,2,8,2304]{4,3,1,2,0:T(8,128)(2,1)S(1)} %dynamic-slice_bitcast_fusion.1), channel_id=1, source_target_pairs={{0,8},{4,28},{8,16},{12,4},{16,24},{20,12},{24,0},{28,20},{1,9},{5... | collective-permute-start | bytes 3538952 | tf_op jit(solution)/shard_map/ppermute | solution.py:55
  344.1 24.2 %collective-permute-start.110 = (bf16[4,4,36,1024]{3,1,2,0:T(4,128)(2,1)}, bf16[4,4,36,1024]{3,1,2,0:T(4,128)(2,1)}, u32[]{:S(2)}, u32[]{:S(2)}) collective-permute-start(bf16[4,4,36,1024]{3,1,2,0:T(4,128)(2,1)} %copy.309), channel_id=1, source_target_pairs={{0,32},{4,100},{32,64},{36,4},{64,96},{68,36},{96,0},{100,68},{1,3... | collective-permute-start | bytes 3538952 | tf_op jit(solution)/shard_map/ppermute | solution.py:55
  345.5 27.2 %collective-permute-start.100 = (bf16[4,4,2,8,2304]{4,3,2,1,0:T(8,128)(2,1)}, bf16[4,4,2,8,2304]{4,3,2,1,0:T(8,128)(2,1)}, u32[]{:S(2)}, u32[]{:S(2)}) collective-permute-start(bf16[4,4,2,8,2304]{4,3,2,1,0:T(8,128)(2,1)} %fusion.6), channel_id=1, source_target_pairs={{0,1},{4,7},{1,2},{5,4},{2,3},{6,5},{3,0},{7,6},{8,9},{12,15},{9,1... | collective-permute-start | bytes 3538952 | tf_op jit(solution)/shard_map/ppermute | solution.py:55
  347.4 29.7 %collective-permute-start.91 = (bf16[4,4,2,8,2304]{4,3,1,2,0:T(8,128)(2,1)}, bf16[4,4,2,8,2304]{4,3,1,2,0:T(8,128)(2,1)}, u32[]{:S(2)}, u32[]{:S(2)}) collective-permute-start(bf16[4,4,2,8,2304]{4,3,1,2,0:T(8,128)(2,1)} %fusion.9), channel_id=1, source_target_pairs={{0,8},{4,28},{8,16},{12,4},{16,24},{20,12},{24,0},{28,20},{1,9},{5... | collective-permute-start | bytes 3538952 | tf_op jit(solution)/shard_map/ppermute | solution.py:55
  363.2 37.1 %collective-permute-start.62 = (f32[256,1024]{1,0:T(8,128)}, f32[256,1024]{1,0:T(8,128)}, u32[]{:S(2)}, u32[]{:S(2)}) collective-permute-start(f32[256,1024]{1,0:T(8,128)} %constant_dynamic-slice_fusion.25), channel_id=1, source_target_pairs={{0,4},{4,0},{1,5},{5,1},{2,6},{6,2},{3,7},{7,3},{8,12},{12,8},{9,1... | collective-permute-start | bytes 3145736 | tf_op jit(solution)/shard_map/ppermute | solution.py:59
  365.3 16.4 %collective-permute-start.81 = (bf16[4,4,8,1280]{3,2,1,0:T(8,128)(2,1)}, bf16[4,4,8,1280]{3,2,1,0:T(8,128)(2,1)S(1)}, u32[]{:S(2)}, u32[]{:S(2)}) collective-permute-start(bf16[4,4,8,1280]{3,2,1,0:T(8,128)(2,1)} %fusion.57), channel_id=1, source_target_pairs={{0,1},{4,7},{1,2},{5,4},{2,3},{6,5},{3,0},{7,6},{8,9},{12,15},{9,1... | collective-permute-start | bytes 983048 | tf_op jit(solution)/shard_map/ppermute | solution.py:55
  368.4 13.7 %collective-permute-start.72 = (bf16[4,4,8,1408]{3,2,0,1:T(8,128)(2,1)S(1)}, bf16[4,4,8,1408]{3,2,0,1:T(8,128)(2,1)S(1)}, u32[]{:S(2)}, u32[]{:S(2)}) collective-permute-start(bf16[4,4,8,1408]{3,2,0,1:T(8,128)(2,1)S(1)} %fusion.41), channel_id=1, source_target_pairs={{0,8},{4,28},{8,16},{12,4},{16,24},{20,12},{24,0},{28,20},{1,9},{5... | collective-permute-start | bytes 1081352 | tf_op jit(solution)/shard_map/ppermute | solution.py:55
  372.7 11.2 %collective-permute-start.63 = (bf16[4,4,8,1408]{3,2,1,0:T(8,128)(2,1)S(1)}, bf16[4,4,8,1408]{3,2,1,0:T(8,128)(2,1)S(1)}, u32[]{:S(2)}, u32[]{:S(2)}) collective-permute-start(bf16[4,4,8,1408]{3,2,1,0:T(8,128)(2,1)S(1)} %fusion.49), channel_id=1, source_target_pairs={{0,32},{4,100},{32,64},{36,4},{64,96},{68,36},{96,0},{100,68},{1,3... | collective-permute-start | bytes 1081352 | tf_op jit(solution)/shard_map/ppermute | solution.py:55
  377.1 115.3 %collective-permute-start.111 = (bf16[4,4,36,1024]{3,1,2,0:T(4,128)(2,1)}, bf16[4,4,36,1024]{3,1,2,0:T(4,128)(2,1)}, u32[]{:S(2)}, u32[]{:S(2)}) collective-permute-start(bf16[4,4,36,1024]{3,1,2,0:T(4,128)(2,1)} %copy.311), channel_id=1, source_target_pairs={{0,32},{4,100},{32,64},{36,4},{64,96},{68,36},{96,0},{100,68},{1,3... | collective-permute-start | bytes 3538952 | tf_op jit(solution)/shard_map/ppermute | solution.py:55
  384.0 14.6 %collective-permute-start.64 = (bf16[4,4,8,1408]{3,2,1,0:T(8,128)(2,1)S(1)}, bf16[4,4,8,1408]{3,2,1,0:T(8,128)(2,1)S(1)}, u32[]{:S(2)}, u32[]{:S(2)}) collective-permute-start(bf16[4,4,8,1408]{3,2,1,0:T(8,128)(2,1)S(1)} %fusion.25), channel_id=1, source_target_pairs={{0,32},{4,100},{32,64},{36,4},{64,96},{68,36},{96,0},{100,68},{1,3... | collective-permute-start | bytes 1081352 | tf_op jit(solution)/shard_map/ppermute | solution.py:55
  390.4 8.9 %collective-permute-start.83 = (bf16[4,4,8,1280]{3,2,1,0:T(8,128)(2,1)S(1)}, bf16[4,4,8,1280]{3,2,1,0:T(8,128)(2,1)S(1)}, u32[]{:S(2)}, u32[]{:S(2)}) collective-permute-start(bf16[4,4,8,1280]{3,2,1,0:T(8,128)(2,1)S(1)} %fusion.30), channel_id=1, source_target_pairs={{0,1},{4,7},{1,2},{5,4},{2,3},{6,5},{3,0},{7,6},{8,9},{12,15},{9,1... | collective-permute-start | bytes 983048 | tf_op jit(solution)/shard_map/ppermute | solution.py:55
  391.8 23.2 %collective-permute-start.74 = (bf16[4,4,8,1408]{3,2,0,1:T(8,128)(2,1)}, bf16[4,4,8,1408]{3,2,0,1:T(8,128)(2,1)}, u32[]{:S(2)}, u32[]{:S(2)}) collective-permute-start(bf16[4,4,8,1408]{3,2,0,1:T(8,128)(2,1)} %fusion.21), channel_id=1, source_target_pairs={{0,8},{4,28},{8,16},{12,4},{16,24},{20,12},{24,0},{28,20},{1,9},{5... | collective-permute-start | bytes 1081352 | tf_op jit(solution)/shard_map/ppermute | solution.py:55
  399.5 9.7 %collective-permute-start.84 = (bf16[4,8,1280]{2,1,0:T(8,128)(2,1)S(1)}, bf16[4,8,1280]{2,1,0:T(8,128)(2,1)S(1)}, u32[]{:S(2)}, u32[]{:S(2)}) collective-permute-start(bf16[4,8,1280]{2,1,0:T(8,128)(2,1)S(1)} %dynamic-slice_bitcast_fusion.8), channel_id=1, source_target_pairs={{0,32},{4,100},{32,64},{36,4},{64,96},{68,36},{96,0},{100,68},{1,3... | collective-permute-start | bytes 245768 | tf_op jit(solution)/shard_map/ppermute | solution.py:55
  412.7 82.0 %collective-permute-start.101 = (bf16[4,4,2,8,2304]{4,3,2,1,0:T(8,128)(2,1)}, bf16[4,4,2,8,2304]{4,3,2,1,0:T(8,128)(2,1)S(1)}, u32[]{:S(2)}, u32[]{:S(2)}) collective-permute-start(bf16[4,4,2,8,2304]{4,3,2,1,0:T(8,128)(2,1)} %fusion.5), channel_id=1, source_target_pairs={{0,1},{4,7},{1,2},{5,4},{2,3},{6,5},{3,0},{7,6},{8,9},{12,15},{9,1... | collective-permute-start | bytes 3538952 | tf_op jit(solution)/shard_map/ppermute | solution.py:55
  412.7 8.8 %collective-permute-start.65 = (bf16[4,4,8,1408]{3,2,1,0:T(8,128)(2,1)}, bf16[4,4,8,1408]{3,2,1,0:T(8,128)(2,1)S(1)}, u32[]{:S(2)}, u32[]{:S(2)}) collective-permute-start(bf16[4,4,8,1408]{3,2,1,0:T(8,128)(2,1)} %fusion.24), channel_id=1, source_target_pairs={{0,32},{4,100},{32,64},{36,4},{64,96},{68,36},{96,0},{100,68},{1,3... | collective-permute-start | bytes 1081352 | tf_op jit(solution)/shard_map/ppermute | solution.py:55
  413.0 16.9 %collective-permute-start.122 = (f32[8,512]{1,0:T(8,128)S(1)}, f32[8,512]{1,0:T(8,128)S(1)}, u32[]{:S(2)}, u32[]{:S(2)}) collective-permute-start(f32[8,512]{1,0:T(8,128)S(1)} %add_add_fusion.2), channel_id=1, source_target_pairs={{0,2},{1,3},{2,0},{3,1},{4,6},{5,7},{6,4},{7,5},{8,10},{9,11},{10,... | collective-permute-start | bytes 49160 | tf_op jit(solution)/shard_map/ppermute | solution.py:95
  415.0 15.7 %collective-permute-start.123 = (f32[8,512]{1,0:T(8,128)S(1)}, f32[8,512]{1,0:T(8,128)S(1)}, u32[]{:S(2)}, u32[]{:S(2)}) collective-permute-start(f32[8,512]{1,0:T(8,128)S(1)} %add_add_fusion.2), channel_id=1, source_target_pairs={{0,1},{1,2},{2,3},{3,0},{4,5},{5,6},{6,7},{7,4},{8,9},{9,10},{10,1... | collective-permute-start | bytes 49160 | tf_op jit(solution)/shard_map/ppermute | solution.py:95
  421.6 9.1 %collective-permute-start.124 = (f32[8,512]{1,0:T(8,128)S(1)}, f32[8,512]{1,0:T(8,128)S(1)}, u32[]{:S(2)}, u32[]{:S(2)}) collective-permute-start(f32[8,512]{1,0:T(8,128)S(1)} %add_add_fusion.2), channel_id=1, source_target_pairs={{0,3},{1,0},{2,1},{3,2},{4,7},{5,4},{6,5},{7,6},{8,11},{9,8},{10,9... | collective-permute-start | bytes 49160 | tf_op jit(solution)/shard_map/ppermute | solution.py:95
  436.0 60.6 %collective-permute-start.92 = (bf16[4,4,2,8,2304]{4,3,1,2,0:T(8,128)(2,1)S(1)}, bf16[4,4,2,8,2304]{4,3,1,2,0:T(8,128)(2,1)S(1)}, u32[]{:S(2)}, u32[]{:S(2)}) collective-permute-start(bf16[4,4,2,8,2304]{4,3,1,2,0:T(8,128)(2,1)S(1)} %copy-done.42), channel_id=1, source_target_pairs={{0,8},{4,28},{8,16},{12,4},{16,24},{20,12},{24,0},{28,20},{1,9},{5... | collective-permute-start | bytes 3538952 | tf_op jit(solution)/shard_map/ppermute | solution.py:55
  442.7 11.7 %collective-permute-start.66 = (bf16[4,8,1408]{2,1,0:T(8,128)(2,1)S(1)}, bf16[4,8,1408]{2,1,0:T(8,128)(2,1)S(1)}, u32[]{:S(2)}, u32[]{:S(2)}) collective-permute-start(bf16[4,8,1408]{2,1,0:T(8,128)(2,1)S(1)} %dynamic-slice_bitcast_fusion.6), channel_id=1, source_target_pairs={{0,8},{4,28},{8,16},{12,4},{16,24},{20,12},{24,0},{28,20},{1,9},{5... | collective-permute-start | bytes 270344 | tf_op jit(solution)/shard_map/ppermute | solution.py:55
  448.7 10.7 %collective-permute-start.76 = (bf16[4,8,1408]{2,1,0:T(8,128)(2,1)S(1)}, bf16[4,8,1408]{2,1,0:T(8,128)(2,1)S(1)}, u32[]{:S(2)}, u32[]{:S(2)}) collective-permute-start(bf16[4,8,1408]{2,1,0:T(8,128)(2,1)S(1)} %fusion.67), channel_id=1, source_target_pairs={{0,1},{4,7},{1,2},{5,4},{2,3},{6,5},{3,0},{7,6},{8,9},{12,15},{9,1... | collective-permute-start | bytes 270344 | tf_op jit(solution)/shard_map/ppermute | solution.py:55
  549.3 11.6 %collective-permute-start.130 = (f32[1,1]{1,0:T(1,128)}, f32[1,1]{1,0:T(1,128)}, u32[]{:S(2)}, u32[]{:S(2)}) collective-permute-start(f32[1,1]{1,0:T(1,128)} %add.936), channel_id=1, source_target_pairs={{0,32},{32,64},{64,96},{96,0},{1,33},{33,65},{65,97},{97,1},{2,34}... | collective-permute-start | bytes 20 | tf_op jit(solution)/shard_map/ppermute | solution.py:95
  550.7 10.2 %collective-permute-start.131 = (f32[1,1]{1,0:T(1,128)}, f32[1,1]{1,0:T(1,128)}, u32[]{:S(2)}, u32[]{:S(2)}) collective-permute-start(f32[1,1]{1,0:T(1,128)} %add.936), channel_id=1, source_target_pairs={{0,96},{32,0},{64,32},{96,64},{1,97},{33,1},{65,33},{97,65},{2,98}... | collective-permute-start | bytes 20 | tf_op jit(solution)/shard_map/ppermute | solution.py:95
  562.1 11.6 %collective-permute-start.133 = (f32[1,1]{1,0:T(1,128)}, f32[1,1]{1,0:T(1,128)}, u32[]{:S(2)}, u32[]{:S(2)}) collective-permute-start(f32[1,1]{1,0:T(1,128)} %add.939), channel_id=1, source_target_pairs={{0,1},{1,2},{2,3},{3,0},{4,5},{5,6},{6,7},{7,4},{8,9},{9,10},{10,1... | collective-permute-start | bytes 20 | tf_op jit(solution)/shard_map/ppermute | solution.py:95
  563.5 10.3 %collective-permute-start.134 = (f32[1,1]{1,0:T(1,128)}, f32[1,1]{1,0:T(1,128)}, u32[]{:S(2)}, u32[]{:S(2)}) collective-permute-start(f32[1,1]{1,0:T(1,128)} %add.939), channel_id=1, source_target_pairs={{0,3},{1,0},{2,1},{3,2},{4,7},{5,4},{6,5},{7,6},{8,11},{9,8},{10,9... | collective-permute-start | bytes 20 | tf_op jit(solution)/shard_map/ppermute | solution.py:95
  575.0 11.6 %collective-permute-start.136 = (f32[1,1]{1,0:T(1,128)}, f32[1,1]{1,0:T(1,128)}, u32[]{:S(2)}, u32[]{:S(2)}) collective-permute-start(f32[1,1]{1,0:T(1,128)} %add.942), channel_id=1, source_target_pairs={{0,8},{8,16},{16,24},{24,0},{1,9},{9,17},{17,25},{25,1},{2,10},{10... | collective-permute-start | bytes 20 | tf_op jit(solution)/shard_map/ppermute | solution.py:95
  576.3 10.3 %collective-permute-start.137 = (f32[1,1]{1,0:T(1,128)}, f32[1,1]{1,0:T(1,128)}, u32[]{:S(2)}, u32[]{:S(2)}) collective-permute-start(f32[1,1]{1,0:T(1,128)} %add.942), channel_id=1, source_target_pairs={{0,24},{8,0},{16,8},{24,16},{1,25},{9,1},{17,9},{25,17},{2,26},{10... | collective-permute-start | bytes 20 | tf_op jit(solution)/shard_map/ppermute | solution.py:95
  (165 other events, 975.9 us)
